TPU v7x, 32 devices: a whole 2x2x4 slice. The times are simulated.
32 devices in a mesh: dp: 16 (over z, x, core), mp: 2 (over y).
Axes of the slice: x: 2, y: 2, z: 4, core: 2. Of those that a mesh axis runs over, the one named last changes fastest.
Arguments:
- queries: bfloat16 [16384, 256], P('dp'), may hold values from -1400 to 1400, as said below
- item_table: bfloat16 [8192, 512], P('dp'), may hold values from -6 to 6
- cand_row: int32 [4096], P('dp'), may hold values from 0 to 511
- cand_owner: int32 [4096, 1], P('dp'), may hold values from 0 to 15; in each aligned block of 256 rows (0 to 255, 256 to 511, ...) at most 32 rows name the same one
- cand_count: int32 [4096], P('dp'), may hold values from 1 to 100
- positive: int32 [16384], P('dp'), may hold values from 0 to 4095
- w_in: bfloat16 [512, 1024], P(None, 'mp'), may hold values from -0.25 to 0.25
- b_in: float32 [1024], P('mp'), may hold values from -3 to 3
- w_out: bfloat16 [1024, 256], P('mp'), may hold values from -0.1875 to 0.1875
Outputs:
- loss: float32 [16384], P('dp')
- query_grad: float32 [16384, 256], P(('dp', 'mp'))
- grad_w_in: float32 [512, 1024], P(None, 'mp')
- grad_b_in: float32 [1024], P('mp')
- grad_w_out: float32 [1024, 256], P('mp')
- grad_table: float32 [8192, 512], P('dp')
Inputs may be any that keep to these rules, and one draw needn't show every extreme that they name: `cand_owner`: no owner is named by more than 32 of the candidates of one index of dp; in some index of dp one owner is named by exactly 32. `queries`: query vectors are finite.
All inputs are finite; a program needn't handle non-finite values.
Results may differ from a plain program's by a relative error of at most 0.01.
Values may be sent and summed in bfloat16 or wider, within the bound.
No kernel may reach another device: no remote copies, remote signals or barrier semaphores. Data moves between devices by JAX's collectives and lax.ppermute only.
A program may use at most 64 MiB of HBM per device.

v0:
```python
import functools
import math

import jax
import jax.numpy as jnp
from jax import lax
from jax.experimental import pallas as pl
from jax.experimental.pallas import tpu as pltpu
from jax.sharding import PartitionSpec as P

F32 = jnp.float32
BF16 = jnp.bfloat16
F16 = jnp.float16
ABSENT = -1e30
COUNT_BASE = 128
WORD_BITS = 22
EXPONENT_BASE = 20
TABLE_MAX = 6.0
W_IN_MAX = 0.25
B_IN_MAX = 3.0
W_OUT_MAX = 0.1875
LIMIT = 32768.0
LOG2E = math.log2(math.e)
GROUP = 16
NT = (((1,), (1,)), ((), ()))
TN = (((0,), (0,)), ((), ()))


def hop(value, bits, axis="dp"):
    size = lax.axis_size(axis)
    return lax.ppermute(value, axis, [(i, i ^ bits) for i in range(size)])


def dot(a, b, dims=None, **kw):
    if dims is None:
        dims = (((1,), (0,)), ((), ()))
    return lax.dot_general(a, b, dims, preferred_element_type=F32, **kw)


def column_bias(bias_ref, first, count):
    lane = first // 128
    return bias_ref[pl.ds(first % 128, count), lane : lane + 1]


def stats_kernel(scale, base, count, last, *refs):
    items_refs, refs = refs[:count], refs[count:]
    qt_ref, bias_ref, m_in_ref, l_in_ref, m_ref, *score_refs = refs
    l_ref = None if last else score_refs.pop(0)
    block = score_refs[0].shape[0]
    old = m_in_ref[...]
    new = old
    for items_ref, score_ref in zip(items_refs, score_refs):
        score_ref[...] = dot(items_ref[0:block], qt_ref[...])
    for n, score_ref in enumerate(score_refs):
        for r in range(0, block, 8):
            bias = column_bias(bias_ref, base + n * block + r, 8)
            score = score_ref[r : r + 8] * scale + bias
            score_ref[r : r + 8] = score
            new = jnp.maximum(new, score)
    total = l_in_ref[...] * jnp.exp2(old - new)
    for score_ref in score_refs:
        for r in range(0, block, 8):
            total = total + jnp.exp2(score_ref[r : r + 8] - new)
    if last:
        top = jnp.max(new, axis=0, keepdims=True)
        m_ref[0:1] = top
        m_ref[1:2] = jnp.sum(total * jnp.exp2(new - top), axis=0, keepdims=True)
    else:
        m_ref[...] = new
        l_ref[...] = total


def in_vmem(count):
    return [pl.BlockSpec(memory_space=pltpu.VMEM)] * count


def run_stats(items, block, qt, bias, m, l, scale, base, last):
    count, nq = len(items), qt.shape[1]
    shapes = [(2, nq)] if last else [(8, nq)] * 2
    return pl.pallas_call(
        functools.partial(stats_kernel, scale, base, count, last),
        in_specs=in_vmem(count + 4),
        out_specs=in_vmem(len(shapes)),
        out_shape=[jax.ShapeDtypeStruct(shape, F32) for shape in shapes],
        scratch_shapes=[pltpu.VMEM((block, nq), F32)] * count,
        compiler_params=pltpu.CompilerParams(vmem_limit_bytes=6 << 20),
    )(*items, qt, bias, m, l)


def lse_kernel(count, index_ref, *refs):
    part_refs, (lse_ref, held_ref) = refs[:count], refs[count:]
    for k in range(count):
        held_ref[index_ref[0] ^ k] = part_refs[k][...]
    parts = [held_ref[k] for k in range(count)]
    top = functools.reduce(jnp.maximum, [p[0:1] for p in parts])
    total = functools.reduce(jnp.add, [p[1:2] * jnp.exp2(p[0:1] - top) for p in parts])
    lse_ref[...] = top + jnp.log2(total)


def run_lse(index, parts):
    nq = parts[0].shape[1]
    return pl.pallas_call(
        functools.partial(lse_kernel, len(parts)),
        in_specs=[pl.BlockSpec(memory_space=pltpu.SMEM)] + in_vmem(len(parts)),
        out_specs=in_vmem(1)[0],
        out_shape=jax.ShapeDtypeStruct((1, nq), F32),
        scratch_shapes=[pltpu.VMEM((len(parts), 2, nq), F32)],
        compiler_params=pltpu.CompilerParams(vmem_limit_bytes=2 << 20),
    )(index, *parts)


def grad_kernel(scale, base, count, add, *refs):
    items_refs, refs = refs[:count], refs[count:]
    more_refs, refs = refs[:add], refs[add:]
    qt_ref, q_ref, bias_ref, lse_ref, pos_ref, qg_in_ref, sp_in_ref, *refs = refs
    sums_refs, (qg_ref, sp_ref, *scratch) = refs[:count], refs[count:]
    score_refs, prob_refs = scratch[:count], scratch[count:]
    block, queries = score_refs[0].shape
    for items_ref, score_ref in zip(items_refs, score_refs):
        score_ref[...] = dot(items_ref[0:block], qt_ref[...])
    down = lax.broadcasted_iota(jnp.int32, (8, queries), 0)
    offset = jnp.broadcast_to(pos_ref[...], (8, queries)) - down
    lse = jnp.broadcast_to(lse_ref[...], (8, queries))
    found = sp_in_ref[...]
    for n in range(count):
        score_ref, prob_ref = score_refs[n], prob_refs[n]
        for r in range(0, block, GROUP):
            pieces = []
            for s in range(r, r + GROUP, 8):
                at = base + n * block + s
                score = score_ref[s : s + 8]
                here = offset == at
                found = found + jnp.where(here, score, 0.0)
                prob = jnp.exp2((score * (scale * LOG2E) + column_bias(bias_ref, at, 8)) - lse)
                pieces.append(jnp.where(here, prob - 1.0, prob))
            prob_ref[r : r + GROUP] = jnp.concatenate(pieces, axis=0).astype(BF16)
        sums = dot(prob_ref[...], q_ref[...]) * scale
        sums_refs[n][...] = sums + more_refs[n][...] if add else sums
        share = dot(items_refs[n][0:block], prob_ref[...], TN)
        qg_ref[...] = (qg_in_ref[...] if n == 0 else qg_ref[...]) + share
    sp_ref[...] = found


def run_grad(items, block, more, qt, q, bias, lse, pos, qg, sp, scale, base):
    count, (width, nq) = len(items), qt.shape
    before = count + len(more)
    *sums, qg, sp = pl.pallas_call(
        functools.partial(grad_kernel, scale, base, count, len(more)),
        in_specs=in_vmem(before + 7),
        out_specs=in_vmem(count + 2),
        out_shape=[jax.ShapeDtypeStruct((block, width), F32)] * count
        + [jax.ShapeDtypeStruct((width, nq), F32), jax.ShapeDtypeStruct((8, nq), F32)],
        scratch_shapes=[pltpu.VMEM((block, nq), F32)] * count
        + [pltpu.VMEM((block, nq), BF16)] * count,
        input_output_aliases={before + 5: count, before + 6: count + 1},
        compiler_params=pltpu.CompilerParams(vmem_limit_bytes=8 << 20),
    )(*items, *more, qt, q, bias, lse, pos, qg, sp)
    return sums, qg, sp


def backward_kernel(count, index_ref, factor_ref, *refs):
    grad_refs, (pre_ref, hidden_ref, emb_ref, w_out_ref) = refs[:count], refs[count : count + 4]
    grad_ref, pre_grad_ref, b_ref, *sums_refs = refs[count + 4 :]
    part = grad_refs[0].shape[0]
    for k in range(count):
        start = pl.multiple_of((index_ref[0] ^ k) * part, part)
        grad_ref[pl.ds(start, part)] = grad_refs[k][...]
    back = dot(grad_ref[...], w_out_ref[...], NT)
    pre_grad = jnp.where(pre_ref[...] > 0.0, back, 0.0).astype(BF16)
    pre_grad_ref[...] = pre_grad
    b_ref[...] = jnp.sum(pre_grad.astype(F32), axis=0, keepdims=True)
    sums_in = dot(emb_ref[...], pre_grad, TN) * factor_ref[0]
    sums_out = dot(hidden_ref[...], grad_ref[...], TN) * factor_ref[1]
    if len(sums_refs) == 1:
        units = sums_in.shape[1]
        sums_refs[0][:, :units] = sums_in
        sums_refs[0][:, units:] = sums_out
    else:
        sums_refs[0][...] = sums_in
        sums_refs[1][...] = sums_out


def run_backward(index, factors, grads, pre, hidden, emb, w_out):
    rows, units = pre.shape
    width_emb, width_out = emb.shape[1], w_out.shape[1]
    if units == width_emb:
        sums = [(width_emb, units + width_out)]
    else:
        sums = [(width_emb, units), (units, width_out)]
    grad, pre_grad, local_b, *sums = pl.pallas_call(
        functools.partial(backward_kernel, len(grads)),
        in_specs=[pl.BlockSpec(memory_space=pltpu.SMEM)] * 2 + in_vmem(len(grads) + 4),
        out_specs=in_vmem(3 + len(sums)),
        out_shape=[
            jax.ShapeDtypeStruct((rows, width_out), BF16),
            jax.ShapeDtypeStruct((rows, units), BF16),
            jax.ShapeDtypeStruct((1, units), F32),
        ]
        + [jax.ShapeDtypeStruct(shape, F32) for shape in sums],
        compiler_params=pltpu.CompilerParams(vmem_limit_bytes=12 << 20),
    )(index, factors, *grads, pre, hidden, emb, w_out)
    if len(sums) > 1:
        sums = [jnp.concatenate([sums[0], sums[1].reshape(width_emb, -1)], axis=1)]
    return grad, pre_grad, local_b, sums[0]


def joined(mine, other, first):
    return jnp.where(
        first,
        jnp.concatenate([mine, other], axis=0),
        jnp.concatenate([other, mine], axis=0),
    )


def per_device(queries, item_table, cand_row, cand_owner, cand_count, positive, w_in, b_in, w_out):
    n_data = lax.axis_size("dp")
    n_model = lax.axis_size("mp")
    n_z = n_data // 4
    me = lax.axis_index("dp")
    my_model = lax.axis_index("mp")
    n_query, width_out = queries.shape
    rows, width_emb = item_table.shape
    units = w_in.shape[1]
    part = rows // n_model
    cand_local = cand_row.shape[0]
    n_cols = n_data * part
    chunk = n_z * part // 2
    scale = 1.0 / math.sqrt(width_out)
    tie = lax.optimization_barrier
    slice_at = functools.partial(lax.dynamic_slice, allow_negative_indices=False)
    core = me & 1
    half_rows = width_emb // 2
    query_part = n_query // n_model
    starts = [(my_model ^ k) * part for k in range(n_model)]
    share_starts = [(my_model ^ k) * query_part for k in range(n_model)]
    half_starts = [(core ^ k) * half_rows for k in range(2)]
    model_index = my_model.astype(jnp.int32).reshape(1)
    core_first = core == 0

    def place(rel):
        return ((rel >> 1) & 1) * (2 * n_z) + (rel & 1) * n_z + (rel >> 2)

    def bit_of(bits):
        return (me // bits) & 1

    pre = dot(item_table, w_in) + b_in[None, :]
    hidden = jnp.maximum(pre, 0.0).astype(BF16)
    partial = dot(hidden, w_out)

    def part_of(value, k):
        return slice_at(value, (starts[k], 0), (part, value.shape[1]))

    outgoing = [part_of(partial, k) for k in range(1, n_model)]
    arrived = [hop(outgoing[k - 1], k, "mp") for k in range(1, n_model)]
    outgoing, queries, cand_row = tie((outgoing, queries, cand_row))
    qt = queries.T
    packed = jnp.concatenate([w_in, w_out.reshape(width_emb, -1)], axis=1)
    piece = slice_at(packed, (half_starts[0], 0), (half_rows, packed.shape[1]))

    largest = jnp.max(jnp.abs(queries)).astype(F32)
    exponent = jnp.floor(jnp.log2(jnp.maximum(largest, 1e-6))).astype(jnp.int32) + 1
    exponent = jnp.clip(exponent + EXPONENT_BASE, 0, 63)
    word = (cand_owner[:, 0] * rows + cand_row) * COUNT_BASE + cand_count
    word = (word + exponent * (1 << WORD_BITS))[None, :]
    words = jnp.concatenate([word, hop(word, 1)], axis=0)
    words = jnp.concatenate([words, hop(words, 2)], axis=0)

    total, arrived, qt, piece = tie((part_of(partial, 0), arrived, qt, piece))
    for other in arrived:
        total = total + other
    size = 4 * cand_local
    digits = jnp.stack([(words.reshape(size) >> shift) & 255 for shift in (0, 8, 16, 24)])
    tail_rows = -(-4 * size // (16 * width_out)) * 16
    digits = jnp.pad(digits.reshape(-1), (0, tail_rows * width_out - 4 * size))
    tail = digits.reshape(tail_rows, width_out).astype(BF16)
    payload = jnp.concatenate([total.astype(BF16), tail], axis=0)

    along_z = {0: payload}
    for j in range(n_z - 1, 0, -1):
        along_z[j] = hop(payload, j << 2)
    along_x = {j: hop(along_z[j], 2) for j in range(2)}
    along_z, along_x = tie((along_z, along_x))
    tails = jnp.stack([along_z[j][part:] for j in range(n_z)]).reshape(n_z, -1)[:, : 4 * size]
    tails = tails.astype(jnp.int32).reshape(n_z, 4, size)
    words = tails[:, 0] + tails[:, 1] * 256 + tails[:, 2] * 65536 + tails[:, 3] * 16777216

    flat = words.reshape(-1)
    n_cand = flat.shape[0]
    q_bound = jnp.exp2((jnp.max(flat >> WORD_BITS) - EXPONENT_BASE).astype(F32))
    flat = flat & ((1 << WORD_BITS) - 1)

    hidden_max = width_emb * TABLE_MAX * W_IN_MAX + B_IN_MAX
    gradient_sum = n_data * n_query * 2.0 * scale
    bounds = [
        2 * n_query * 2.0 * scale,
        4 * n_query * 2.0 * scale,
        gradient_sum * width_out * W_OUT_MAX * TABLE_MAX,
        gradient_sum * hidden_max,
    ]
    factors = [(LIMIT / bound) / q_bound for bound in bounds]
    growths = [q_bound * (bound / LIMIT) for bound in bounds]
    row = (flat // COUNT_BASE) % rows
    column = place((flat // (COUNT_BASE * rows)) ^ me) * part + row % part
    column = jnp.where(row // part == my_model, column, -1)
    share = 1.0 / (flat % COUNT_BASE).astype(F32)
    lanes = 128
    high = (jnp.arange(n_cols // lanes)[:, None] == (column >> 7)[None, :]).astype(F32)
    low = jnp.where(jnp.arange(lanes)[:, None] == (column & 127)[None, :], share[None, :], 0.0)
    weight = dot(low, high, NT, precision=lax.Precision.HIGHEST)
    bias = jnp.where(weight > 0.0, jnp.log2(weight), ABSENT)
    own_mask = dot(item_table, packed[:, :units]) + b_in[None, :] > 0.0
    bias, factors, growths, share_starts, half_starts, model_index, core_first, own_mask = tie(
        (bias, factors, growths, share_starts, half_starts, model_index, core_first, own_mask)
    )

    spot = ((positive // cand_local) ^ me) * cand_local + positive % cand_local
    side = 64
    table = flat.reshape(n_cand // side, side)
    digits = jnp.concatenate([table & 255, (table >> 8) & 255, table >> 16], axis=1).astype(BF16)
    picked = (jnp.arange(n_cand // side)[:, None] == (spot // side)[None, :]).astype(BF16)
    found = dot(digits, picked, TN).reshape(3, side, n_query)
    mine = jnp.arange(side)[:, None] == (spot % side)[None, :]
    digit = jnp.sum(jnp.where(mine[None], found, 0.0), axis=1).astype(jnp.int32)
    pos_word = digit[0] + digit[1] * 256 + digit[2] * 65536
    pos_row = (pos_word // COUNT_BASE) % rows
    pos_col = place((pos_word // (COUNT_BASE * rows)) ^ me) * part + pos_row % part
    pos_col = jnp.where(pos_row // part == my_model, pos_col, -1)[None, :]
    pos_logc = jnp.log((pos_word % COUNT_BASE).astype(F32))

    halves = [range(h * n_z // 2, (h + 1) * n_z // 2) for h in range(2)]
    start_of = {
        (x, c, h): ((x * 2 + c) * 2 + h) * chunk for x in range(2) for c in range(2) for h in range(2)
    }
    items = {}
    m8 = jnp.full((8, n_query), ABSENT, F32)
    l8 = jnp.zeros((8, n_query), F32)

    def gathered(x, h, blocks):
        items[x, 0, h] = [blocks[j] for j in halves[h]]
        items[x, 1, h] = [hop(v, 1) for v in items[x, 0, h]]

    def statistics(m, l, *chosen):
        for key in chosen:
            m, l = run_stats(items[key], part, qt, bias, m, l, scale * LOG2E, start_of[key], False)
        return m, l

    for j in range(2, n_z):
        along_x[j] = hop(along_z[j], 2)
    gathered(0, 0, along_z)
    m8, l8 = statistics(m8, l8, (0, 0, 0), (0, 1, 0))
    along_x, m8, l8 = tie((along_x, m8, l8))
    gathered(0, 1, along_z)
    m8, l8 = statistics(m8, l8, (0, 0, 1), (0, 1, 1))
    gathered(1, 0, along_x)
    m8, l8 = statistics(m8, l8, (1, 0, 0))
    gathered(1, 1, along_x)
    m8, l8 = statistics(m8, l8, (1, 1, 0), (1, 0, 1))
    (local,) = run_stats(
        items[1, 1, 1], part, qt, bias, m8, l8, scale * LOG2E, start_of[1, 1, 1], True
    )
    lse = run_lse(model_index, [local] + [hop(local, k, "mp") for k in range(1, n_model)])

    piece, b_late, lse = tie((piece, b_in[None, :], lse))
    others = [(hop(piece, k, "mp"), hop(b_late, k, "mp")) for k in range(1, n_model)]

    qg = jnp.zeros((width_out, n_query), F32)
    sp = jnp.zeros((8, n_query), F32)
    chip_sums, crossed, z_sums = {}, {}, [None] * n_z

    def gradients(key, qg, sp, more=()):
        return run_grad(
            items[key], part, more, qt, queries, bias, lse, pos_col, qg, sp,
            scale, start_of[key],
        )

    siblings, crossing = {}, {}
    for h in (1, 0):
        sums, qg, sp = gradients((1, 1, h), qg, sp)
        siblings[1, h] = [hop(v, 1) for v in sums]
    for h in (1, 0):
        chip_sums[1, h], qg, sp = gradients((1, 0, h), qg, sp, siblings[1, h])
        crossing[h], qg = tie(
            ((jnp.concatenate(chip_sums[1, h], axis=0) * factors[0]).astype(F16), qg)
        )
        crossed[h] = hop(crossing[h], 2)
    for h in (1, 0):
        sums, qg, sp = gradients((0, 1, h), qg, sp)
        siblings[0, h] = [hop(v, 1) for v in sums]
    for h in (1, 0):
        crossed[h], qg = tie((crossed[h], qg))
        chip_sums[0, h], qg, sp = gradients((0, 0, h), qg, sp, siblings[0, h])
        for j in range(n_z // 2):
            over = crossed[h][j * part : (j + 1) * part].astype(F32) * growths[0]
            z_sums[h * n_z // 2 + j] = chip_sums[0, h][j] + over
    own_sum = z_sums[0]
    for j in range(n_z - 1, 0, -1):
        sent = hop((z_sums[j] * factors[1]).astype(F16), j << 2)
        own_sum = own_sum + sent.astype(F32) * growths[1]
    own_grad, others = tie((own_sum.astype(BF16), others))
    others = [(joined(got, hop(got, 1), core_first), b) for got, b in others]
    weights = [(packed, b_in[None, :])] + others
    if n_model > 2:
        turn = jnp.arange(n_model) ^ my_model
        stacks = [jnp.take(jnp.stack(group), turn, axis=0) for group in zip(*weights)]
        weights = [(stacks[0][k], stacks[1][k]) for k in range(n_model)]
    weights = [(w[:, :units], w[:, units:].reshape(units, width_out), b) for w, b in weights]
    masks = [dot(item_table, share_in) + b > 0.0 for share_in, _, b in weights]
    if n_model == 2:
        masks[0] = own_mask


    grads = [own_grad] + [hop(own_grad, k, "mp") for k in range(1, n_model)]
    grads, masks = tie((grads, masks))
    item_grad, pre_grad, local_b, value = run_backward(
        model_index, jnp.stack(factors[2:]), grads, pre, hidden, item_table, w_out
    )

    width = value.shape[1]
    keep, give = (slice_at(value, (half_starts[k], 0), (half_rows, width)) for k in range(2))
    bias_steps = [1 << n for n in range(n_data.bit_length() - 1)]
    bias_steps = bias_steps[:1] + bias_steps[:0:-1]

    def step_bias(value, steps):
        for _ in range(min(steps, len(bias_steps))):
            bits = bias_steps.pop(0)
            value = value + hop(value, bits)
        return value

    value = (keep + hop(give.astype(F16), 1).astype(F32)).astype(F16)
    value, local_b = tie((value, step_bias(local_b, 1)))
    chips = n_data // 2
    groups = [[2 * chip + c for chip in range(chips)] for c in range(2)]

    def exchange(blocks):
        return lax.all_to_all(
            blocks, "dp", split_axis=0, concat_axis=0, axis_index_groups=groups, tiled=True
        )

    size = half_rows // chips
    grad_table = None
    for (share_in, share_out, _), mask in zip(weights, masks):
        back = jnp.where(mask, dot(item_grad, share_out, NT), 0.0).astype(BF16)
        term = dot(back, share_in, NT)
        grad_table = term if grad_table is None else grad_table + term

    pieces = exchange(value.reshape(chips, size, width))
    pieces, grad_table = tie((pieces, grad_table))
    total = jnp.sum(pieces.astype(F32), axis=0).astype(F16)
    total, local_b = tie((total, step_bias(local_b, 9)))
    own_half = exchange(jnp.broadcast_to(total[None], (chips, size, width)))
    own_half = own_half.reshape(half_rows, width)

    local_b, qg, sp = tie((local_b, qg, sp))

    item_max = n_model * units * hidden_max * W_OUT_MAX
    q_factor = LIMIT / (2.0 * item_max)
    sp1 = jnp.sum(sp, axis=0)[None, :]
    qg_parts = [
        slice_at(qg, (0, share_starts[k]), (width_out, query_part))
        for k in range(n_model)
    ]
    pos_score, query_sum = sp1, qg_parts[0]
    for k in range(1, n_model):
        sent = hop((qg_parts[k] * q_factor).astype(F16), k, "mp")
        query_sum = query_sum + sent.astype(F32) * (1.0 / q_factor)
        pos_score = pos_score + hop(sp1, k, "mp")
    loss = lse[0] * (1.0 / LOG2E) - (pos_score[0] * scale - pos_logc)
    query_grad = (query_sum * scale).T

    sides = [own_half, hop(own_half, 1)]
    sides_in = [v[:, :units].astype(F32) * growths[2] for v in sides]
    sides_out = [v[:, units:].astype(F32) * growths[3] for v in sides]
    grad_w_in = joined(*sides_in, core_first)
    grad_w_out = joined(*sides_out, core_first).reshape(units, width_out)
    return (loss, query_grad, grad_w_in, local_b[0], grad_w_out, grad_table)


def solution(mesh):
    placed = (
        P("dp", None),
        P("dp", None),
        P("dp"),
        P("dp", None),
        P("dp"),
        P("dp"),
        P(None, "mp"),
        P("mp"),
        P("mp", None),
    )
    return jax.shard_map(
        per_device,
        mesh=mesh,
        in_specs=placed,
        out_specs=(
            P("dp"),
            P(("dp", "mp"), None),
            P(None, "mp"),
            P("mp"),
            P("mp", None),
            P("dp", None),
        ),
        check_vma=False,
    )
```

profile of v0, /device:TPU:0, one launch (start us, length us, event | category | flops | bytes accessed | tf_op | source)
XLA Modules:
  0.0 132.8 jit_solution(9826985719207450344)
XLA Ops:
  0.6 1.7 %maximum_convert_fusion = (bf16[512,512]{1,0:T(8,128)(2,1)S(1)}, f32[512,512]{1,0:T(8,128)S(1)}) fusion(f32[512]{0:T(512)} %param.16, bf16[512,512]{1,0:T(8,128)(2,1)} %refs_4_.1, bf16[512,512]{1,0:T(8,128)(2,1)} %param.15), kind=kOutput, calls=%fused_computation.14 | convolution fusion | flops 269221888 | bytes 2623488 | tf_op jit(solution)/shard_map/dot_general | solution.py:37
  3.5 3.0 %collective-permute-start = (f32[256,256]{1,0:T(8,128)S(1)}, f32[256,256]{1,0:T(8,128)S(1)}, u32[]{:S(2)}, u32[]{:S(2)}) collective-permute-start(f32[256,256]{1,0:T(8,128)S(1)} %get-tuple-element.244), channel_id=1, source_target_pairs={{0,1},{1,0},{2,3},{3,2},{4,5},{5,4},{6,7},{7,6},{8,9},{9,8},{10,11... | collective-permute-start | bytes 786440 | tf_op jit(solution)/shard_map/ppermute | solution.py:31
  9.2 1.6 %collective-permute-start.2 = (s32[2,256]{1,0:T(2,128)S(1)}, s32[2,256]{1,0:T(2,128)S(1)}, u32[]{:S(2)}, u32[]{:S(2)}) collective-permute-start(s32[2,256]{1,0:T(2,128)S(1)} %pad_add_fusion.1), channel_id=1, source_target_pairs={{0,4},{2,6},{4,0},{6,2},{8,12},{10,14},{12,8},{14,10},{16,20},{18,... | collective-permute-start | bytes 6152 | tf_op jit(solution)/shard_map/ppermute | solution.py:31
  11.8 1.1 collective-permute-done.2
  13.1 1.7 %collective-permute-start.3 = (bf16[272,256]{1,0:T(8,128)(2,1)S(1)}, bf16[272,256]{1,0:T(8,128)(2,1)S(1)}, u32[]{:S(2)}, u32[]{:S(2)}) collective-permute-start(bf16[272,256]{1,0:T(8,128)(2,1)S(1)} %pad_maximum_fusion.refs_0_), channel_id=1, source_target_pairs={{0,8},{2,10},{4,12},{6,14},{8,0},{10,2},{12,4},{14,6},{16,24},{18,... | collective-permute-start | bytes 417800 | tf_op jit(solution)/shard_map/ppermute | solution.py:31
  14.8 2.7 %collective-permute-start.4 = (bf16[272,256]{1,0:T(8,128)(2,1)S(1)}, bf16[272,256]{1,0:T(8,128)(2,1)S(1)}, u32[]{:S(2)}, u32[]{:S(2)}) collective-permute-start(bf16[272,256]{1,0:T(8,128)(2,1)S(1)} %pad_maximum_fusion.refs_0_), channel_id=1, source_target_pairs={{0,16},{2,18},{4,20},{6,22},{8,24},{10,26},{12,28},{14,30},{16,0},... | collective-permute-start | bytes 417800 | tf_op jit(solution)/shard_map/ppermute | solution.py:31
  17.6 1.6 %collective-permute-start.6 = (bf16[272,256]{1,0:T(8,128)(2,1)S(1)}, bf16[272,256]{1,0:T(8,128)(2,1)S(1)}, u32[]{:S(2)}, u32[]{:S(2)}) collective-permute-start(bf16[272,256]{1,0:T(8,128)(2,1)S(1)} %pad_maximum_fusion.refs_0_), channel_id=1, source_target_pairs={{0,4},{2,6},{4,0},{6,2},{8,12},{10,14},{12,8},{14,10},{16,20},{18,... | collective-permute-start | bytes 417800 | tf_op jit(solution)/shard_map/ppermute | solution.py:31
  19.7 1.6 %collective-permute-start.7 = (bf16[272,256]{1,0:T(8,128)(2,1)S(1)}, bf16[272,256]{1,0:T(8,128)(2,1)S(1)}, u32[]{:S(2)}, u32[]{:S(2)}) collective-permute-start(bf16[272,256]{1,0:T(8,128)(2,1)S(1)} %collective-permute-done.3.refs_1_), channel_id=1, source_target_pairs={{0,4},{2,6},{4,0},{6,2},{8,12},{10,14},{12,8},{14,10},{16,20},{18,... | collective-permute-start | bytes 417800 | tf_op jit(solution)/shard_map/ppermute | solution.py:31
  21.4 6.5 %collective-permute-done.4.refs_0_ = bf16[272,256]{1,0:T(8,128)(2,1)S(1)} collective-permute-done((bf16[272,256]{1,0:T(8,128)(2,1)S(1)}, bf16[272,256]{1,0:T(8,128)(2,1)S(1)}, u32[]{:S(2)}, u32[]{:S(2)}) %collective-permute-start.4) | collective-permute-done | bytes 139296 | tf_op jit(solution)/shard_map/ppermute | solution.py:31
  29.4 1.5 %collective-permute-start.8 = (bf16[272,256]{1,0:T(8,128)(2,1)S(1)}, bf16[272,256]{1,0:T(8,128)(2,1)}, u32[]{:S(2)}, u32[]{:S(2)}) collective-permute-start(bf16[272,256]{1,0:T(8,128)(2,1)S(1)} %collective-permute-done.4.refs_0_), channel_id=1, source_target_pairs={{0,4},{2,6},{4,0},{6,2},{8,12},{10,14},{12,8},{14,10},{16,20},{18,... | collective-permute-start | bytes 417800 | tf_op jit(solution)/shard_map/ppermute | solution.py:31
  32.6 1.3 multiply_select_fusion.refs_3_.refs_4_.refs_6_
  35.7 1.7 %shard_map.137 = (f32[8,1024]{1,0:T(8,128)S(1)}, f32[8,1024]{1,0:T(8,128)S(1)}) custom-call(bf16[272,256]{1,0:T(8,128)(2,1)S(1)} %collective-permute-done.10.refs_0_, bf16[272,256]{1,0:T(8,128)(2,1)} %collective-permute-done.11.refs_1_, bf16[256,1024]{1,0:T(8,128)(2,1)S(1)} %bitcast.80, f32[128,32]{1,0:T(8,128)S(1)} %multiply_select_fusion.refs_3_.refs_4_.refs_6_, ...), custom_call_target="tpu_custom_call" | custom-call | tf_op jit(solution)/shard_map/pallas_call | solution.py:80
  40.1 1.7 %shard_map.139 = (f32[8,1024]{1,0:T(8,128)S(1)}, f32[8,1024]{1,0:T(8,128)S(1)}) custom-call(bf16[272,256]{1,0:T(8,128)(2,1)} %collective-permute-done.16.refs_0_, bf16[272,256]{1,0:T(8,128)(2,1)S(1)} %collective-permute-done.17.refs_1_, bf16[256,1024]{1,0:T(8,128)(2,1)S(1)} %bitcast.82, f32[128,32]{1,0:T(8,128)S(1)} %multiply_select_fusion.refs_3_.refs_4_.refs_6_, ...), custom_call_target="tpu_custom_call" | custom-call | tf_op jit(solution)/shard_map/pallas_call | solution.py:80
  43.4 1.7 %shard_map.142 = (f32[8,1024]{1,0:T(8,128)S(1)}, f32[8,1024]{1,0:T(8,128)S(1)}) custom-call(bf16[272,256]{1,0:T(8,128)(2,1)} %collective-permute-done.8.refs_0_, bf16[272,256]{1,0:T(8,128)(2,1)} %collective-permute-done.9.refs_1_, bf16[256,1024]{1,0:T(8,128)(2,1)S(1)} %bitcast.85, f32[128,32]{1,0:T(8,128)S(1)} %multiply_select_fusion.refs_3_.refs_4_.refs_6_, ...), custom_call_target="tpu_custom_call" | custom-call | tf_op jit(solution)/shard_map/pallas_call | solution.py:80
  45.9 1.3 collective-permute-start.18
  47.2 2.3 %collective-permute-done.18.refs_1_ = f32[2,1024]{1,0:T(2,128)S(1)} collective-permute-done((f32[2,1024]{1,0:T(2,128)S(1)}, f32[2,1024]{1,0:T(2,128)S(1)}, u32[]{:S(2)}, u32[]{:S(2)}) %collective-permute-start.18) | collective-permute-done | bytes 8224 | tf_op jit(solution)/shard_map/ppermute | solution.py:31
  49.7 1.5 %shard_map.145 = (f32[256,256]{1,0:T(8,128)S(1)}, f32[256,256]{1,0:T(8,128)S(1)}, f32[256,1024]{1,0:T(8,128)S(1)}, f32[8,1024]{1,0:T(8,128)S(1)}) custom-call(bf16[272,256]{1,0:T(8,128)(2,1)S(1)} %collective-permute-done.12.refs_0_, bf16[272,256]{1,0:T(8,128)(2,1)S(1)} %collective-permute-done.13.refs_1_, ...), custom_call_target="tpu_custom_call", output_to_operand_aliasing={{2}: (7, {}), {3}: (8, {})} | custom-call | tf_op jit(solution)/shard_map/pallas_call | solution.py:147
  51.8 1.3 shard_map.146
  53.8 2.3 %shard_map.147 = (f32[256,256]{1,0:T(8,128)S(1)}, f32[256,256]{1,0:T(8,128)S(1)}, f32[256,1024]{1,0:T(8,128)S(1)}, f32[8,1024]{1,0:T(8,128)S(1)}) custom-call(bf16[272,256]{1,0:T(8,128)(2,1)} %collective-permute-done.8.refs_0_, bf16[272,256]{1,0:T(8,128)(2,1)} %collective-permute-done.9.refs_1_, ...), custom_call_target="tpu_custom_call", output_to_operand_aliasing={{2}: (9, {}), {3}: (10, {})} | custom-call | tf_op jit(solution)/shard_map/pallas_call | solution.py:147
  56.1 1.6 %collective-permute-start.28 = (f16[512,256]{1,0:T(8,128)(2,1)S(1)}, f16[512,256]{1,0:T(8,128)(2,1)S(1)}, u32[]{:S(2)}, u32[]{:S(2)}) collective-permute-start(f16[512,256]{1,0:T(8,128)(2,1)S(1)} %fusion.12), channel_id=1, source_target_pairs={{0,4},{2,6},{4,0},{6,2},{8,12},{10,14},{12,8},{14,10},{16,20},{18,... | collective-permute-start | bytes 786440 | tf_op jit(solution)/shard_map/ppermute | solution.py:31
  57.7 1.3 shard_map.148
  59.1 2.2 %shard_map.149 = (f32[256,256]{1,0:T(8,128)S(1)}, f32[256,256]{1,0:T(8,128)S(1)}, f32[256,1024]{1,0:T(8,128)S(1)}, f32[8,1024]{1,0:T(8,128)S(1)}) custom-call(bf16[272,256]{1,0:T(8,128)(2,1)} %collective-permute-done.16.refs_0_, bf16[272,256]{1,0:T(8,128)(2,1)S(1)} %collective-permute-done.17.refs_1_, ...), custom_call_target="tpu_custom_call", output_to_operand_aliasing={{2}: (7, {}), {3}: (8, {})} | custom-call | tf_op jit(solution)/shard_map/pallas_call | solution.py:147
  62.5 2.2 %shard_map.150 = (f32[256,256]{1,0:T(8,128)S(1)}, f32[256,256]{1,0:T(8,128)S(1)}, f32[256,1024]{1,0:T(8,128)S(1)}, f32[8,1024]{1,0:T(8,128)S(1)}) custom-call(bf16[272,256]{1,0:T(8,128)(2,1)S(1)} %copy-done.18, bf16[272,256]{1,0:T(8,128)(2,1)} %collective-permute-done.11.refs_1_, ...), custom_call_target="tpu_custom_call", output_to_operand_aliasing={{2}: (7, {}), {3}: (8, {})} | custom-call | tf_op jit(solution)/shard_map/pallas_call | solution.py:147
  65.3 1.2 collective-permute-start.32
  66.5 1.3 %shard_map.151 = (f32[256,256]{1,0:T(8,128)S(1)}, f32[256,256]{1,0:T(8,128)S(1)}, f32[256,1024]{1,0:T(8,128)S(1)}, f32[8,1024]{1,0:T(8,128)S(1)}) custom-call(bf16[272,256]{1,0:T(8,128)(2,1)S(1)} %copy-done.10, bf16[272,256]{1,0:T(8,128)(2,1)S(1)} %copy-done.12, ...), custom_call_target="tpu_custom_call", output_to_operand_aliasing={{2}: (9, {}), {3}: (10, {})} | custom-call | tf_op jit(solution)/shard_map/pallas_call | solution.py:147
  68.0 2.5 %collective-permute-start.29 = (f16[256,256]{1,0:T(8,128)(2,1)S(1)}, f16[256,256]{1,0:T(8,128)(2,1)S(1)}, u32[]{:S(2)}, u32[]{:S(2)}) collective-permute-start(f16[256,256]{1,0:T(8,128)(2,1)S(1)} %get-tuple-element.246), channel_id=1, source_target_pairs={{0,24},{2,26},{4,28},{6,30},{8,16},{10,18},{12,20},{14,22},{16,8},... | collective-permute-start | bytes 393224 | tf_op jit(solution)/shard_map/ppermute | solution.py:31
  70.5 2.8 %collective-permute-start.30 = (f16[256,256]{1,0:T(8,128)(2,1)S(1)}, f16[256,256]{1,0:T(8,128)(2,1)S(1)}, u32[]{:S(2)}, u32[]{:S(2)}) collective-permute-start(f16[256,256]{1,0:T(8,128)(2,1)S(1)} %get-tuple-element.247), channel_id=1, source_target_pairs={{0,16},{2,18},{4,20},{6,22},{8,24},{10,26},{12,28},{14,30},{16,0},... | collective-permute-start | bytes 393224 | tf_op jit(solution)/shard_map/ppermute | solution.py:31
  73.3 1.3 %shard_map.152 = (f32[256,256]{1,0:T(8,128)S(1)}, f32[256,256]{1,0:T(8,128)S(1)}, f32[256,1024]{1,0:T(8,128)S(1)}, f32[8,1024]{1,0:T(8,128)S(1)}) custom-call(bf16[272,256]{1,0:T(8,128)(2,1)S(1)} %copy-done.6, bf16[272,256]{1,0:T(8,128)(2,1)S(1)} %copy-done.8, ...), custom_call_target="tpu_custom_call", output_to_operand_aliasing={{2}: (9, {}), {3}: (10, {})} | custom-call | tf_op jit(solution)/shard_map/pallas_call | solution.py:147
  74.8 1.3 collective-permute-start.33
  76.1 7.1 %collective-permute-done.30 = f16[256,256]{1,0:T(8,128)(2,1)S(1)} collective-permute-done((f16[256,256]{1,0:T(8,128)(2,1)S(1)}, f16[256,256]{1,0:T(8,128)(2,1)S(1)}, u32[]{:S(2)}, u32[]{:S(2)}) %collective-permute-start.30) | collective-permute-done | bytes 131104 | tf_op jit(solution)/shard_map/ppermute | solution.py:31
  85.4 1.2 fusion.3
  86.6 2.7 %collective-permute-done.34.refs_1_ = bf16[256,256]{1,0:T(8,128)(2,1)S(1)} collective-permute-done((bf16[256,256]{1,0:T(8,128)(2,1)S(1)}, bf16[256,256]{1,0:T(8,128)(2,1)S(1)}, u32[]{:S(2)}, u32[]{:S(2)}) %collective-permute-start.34) | collective-permute-done | bytes 131104 | tf_op jit(solution)/shard_map/ppermute | solution.py:31
  89.4 1.8 %shard_map.153 = (bf16[512,256]{1,0:T(8,128)(2,1)S(1)}, bf16[512,512]{1,0:T(8,128)(2,1)}, f32[1,512]{1,0:T(1,128)S(1)}, f32[512,768]{1,0:T(8,128)S(1)}) custom-call(s32[1]{0:T(128)} %bitcast.4.index_ref, f32[2]{0:T(128)S(1)} %pad_maximum_fusion.2.factor_ref, bf16[256,256]{1,0:T(8,128)(2,1)S(1)} %add_convert_fusion.1.refs_0_, ...), custom_call_target="tpu_custom_call" | custom-call | tf_op jit(solution)/shard_map/pallas_call | solution.py:190
  91.9 1.2 collective-permute-done.37
  94.0 5.7 %all-to-all-start = ((f16[8,32,768]{2,1,0:T(8,128)(2,1)}), f16[8,32,768]{2,1,0:T(8,128)(2,1)}, u32[]{:S(2)}, u32[]{:S(2)}) async-start(f16[8,32,768]{2,1,0:T(8,128)(2,1)} %bitcast.11), calls=%async_computation | async-start | bytes 786432 | tf_op jit(solution)/shard_map/all_to_all | solution.py:435
  99.8 2.1 %collective-permute-start.39 = (f32[1,512]{1,0:T(1,128)S(1)}, f32[1,512]{1,0:T(1,128)S(1)}, u32[]{:S(2)}, u32[]{:S(2)}) collective-permute-start(f32[1,512]{1,0:T(1,128)S(1)} %add.335), channel_id=1, source_target_pairs={{0,8},{2,10},{4,12},{6,14},{8,0},{10,2},{12,4},{14,6},{16,24},{18,... | collective-permute-start | bytes 6152 | tf_op jit(solution)/shard_map/ppermute | solution.py:31
  101.8 1.6 %fusion.7 = f32[512,512]{1,0:T(8,128)S(1)} fusion(bf16[512,512]{1,0:T(8,128)(2,1)S(1)} %copy-done.20, pred[512,512]{1,0:T(32,128)(4,1)} %broadcast_compare_fusion, bf16[512,256]{1,0:T(8,128)(2,1)S(1)} %get-tuple-element.210, bf16[512,256]{1,0:T(8,128)(2,1)S(1)} %copy-done.3), kind=kOutput, calls=%fused_computation.22 | convolution fusion | flops 403177472 | bytes 2359296 | tf_op jit(solution)/shard_map/dot_general | solution.py:37
  103.4 3.0 %collective-permute-done.39 = f32[1,512]{1,0:T(1,128)S(1)} collective-permute-done((f32[1,512]{1,0:T(1,128)S(1)}, f32[1,512]{1,0:T(1,128)S(1)}, u32[]{:S(2)}, u32[]{:S(2)}) %collective-permute-start.39) | collective-permute-done | bytes 2080 | tf_op jit(solution)/shard_map/ppermute | solution.py:31
  106.4 1.6 %collective-permute-start.40 = (f32[1,512]{1,0:T(1,128)S(1)}, f32[1,512]{1,0:T(1,128)S(1)}, u32[]{:S(2)}, u32[]{:S(2)}) collective-permute-start(f32[1,512]{1,0:T(1,128)S(1)} %add.336), channel_id=1, source_target_pairs={{0,4},{2,6},{4,0},{6,2},{8,12},{10,14},{12,8},{14,10},{16,20},{18,... | collective-permute-start | bytes 6152 | tf_op jit(solution)/shard_map/ppermute | solution.py:31
  108.1 2.7 %convolution_add_fusion.1 = f32[512,512]{1,0:T(8,128)} fusion(f32[512,512]{1,0:T(8,128)S(1)} %fusion.7, pred[512,512]{1,0:T(32,128)(4,1)S(1)} %copy-done.23, bf16[512,256]{1,0:T(8,128)(2,1)S(1)} %get-tuple-element.210, bf16[512,768]{1,0:T(8,128)(2,1)} %copy-done.21), kind=kOutput, calls=%fused_computation.4 | convolution fusion | flops 403439616 | bytes 3407872 | tf_op jit(solution)/shard_map/dot_general | solution.py:37
  111.5 1.1 convert_reduce_fusion
  113.4 5.6 %all-to-all-start.1 = ((f16[8,32,768]{2,1,0:T(8,128)(2,1)}), f16[8,32,768]{2,1,0:T(8,128)(2,1)S(1)}, u32[]{:S(2)}, u32[]{:S(2)}) async-start(f16[8,32,768]{2,1,0:T(8,128)(2,1)} %broadcast_in_dim.79), calls=%async_computation.1 | async-start | bytes 786432 | tf_op jit(solution)/shard_map/all_to_all | solution.py:435
  120.2 1.3 collective-permute-start.42
  121.4 1.4 %collective-permute-done.41 = f32[1,1024]{1,0:T(1,128)S(1)} collective-permute-done((f32[1,1024]{1,0:T(1,128)S(1)}, f32[1,1024]{1,0:T(1,128)S(1)}, u32[]{:S(2)}, u32[]{:S(2)}) %collective-permute-start.41) | collective-permute-done | bytes 4128 | tf_op jit(solution)/shard_map/ppermute | solution.py:31
  123.4 3.1 %collective-permute-done.42 = f16[256,512]{1,0:T(8,128)(2,1)S(1)} collective-permute-done((f16[256,512]{1,0:T(8,128)(2,1)S(1)}, f16[256,512]{1,0:T(8,128)(2,1)S(1)}, u32[]{:S(2)}, u32[]{:S(2)}) %collective-permute-start.42) | collective-permute-done | bytes 262176 | tf_op jit(solution)/shard_map/ppermute | solution.py:31
  127.8 1.3 all-to-all-done.1
  129.2 1.6 %collective-permute-done.43 = f16[256,768]{1,0:T(8,128)(2,1)S(1)} collective-permute-done((f16[256,768]{1,0:T(8,128)(2,1)S(1)}, f16[256,768]{1,0:T(8,128)(2,1)S(1)}, u32[]{:S(2)}, u32[]{:S(2)}) %collective-permute-start.43) | collective-permute-done | bytes 393248 | tf_op jit(solution)/shard_map/ppermute | solution.py:31
  131.7 1.1 maximum_select_fusion
  (198 shorter events, 26.6 us)
Async XLA Ops:
  3.5 9.5 %collective-permute-start = (f32[256,256]{1,0:T(8,128)S(1)}, f32[256,256]{1,0:T(8,128)S(1)}, u32[]{:S(2)}, u32[]{:S(2)}) collective-permute-start(f32[256,256]{1,0:T(8,128)S(1)} %get-tuple-element.244), channel_id=1, source_target_pairs={{0,1},{1,0},{2,3},{3,2},{4,5},{5,4},{6,7},{7,6},{8,9},{9,8},{10,11... | collective-permute-start | bytes 786440 | tf_op jit(solution)/shard_map/ppermute | solution.py:31
  8.0 1.2 collective-permute-start.1
  9.2 3.7 %collective-permute-start.2 = (s32[2,256]{1,0:T(2,128)S(1)}, s32[2,256]{1,0:T(2,128)S(1)}, u32[]{:S(2)}, u32[]{:S(2)}) collective-permute-start(s32[2,256]{1,0:T(2,128)S(1)} %pad_add_fusion.1), channel_id=1, source_target_pairs={{0,4},{2,6},{4,0},{6,2},{8,12},{10,14},{12,8},{14,10},{16,20},{18,... | collective-permute-start | bytes 6152 | tf_op jit(solution)/shard_map/ppermute | solution.py:31
  13.1 21.6 %copy-start.5 = (bf16[272,256]{1,0:T(8,128)(2,1)}, bf16[272,256]{1,0:T(8,128)(2,1)S(1)}, u32[]{:S(2)}) copy-start(bf16[272,256]{1,0:T(8,128)(2,1)S(1)} %pad_maximum_fusion.refs_0_) | copy-start | bytes 417796
  13.1 6.7 %collective-permute-start.3 = (bf16[272,256]{1,0:T(8,128)(2,1)S(1)}, bf16[272,256]{1,0:T(8,128)(2,1)S(1)}, u32[]{:S(2)}, u32[]{:S(2)}) collective-permute-start(bf16[272,256]{1,0:T(8,128)(2,1)S(1)} %pad_maximum_fusion.refs_0_), channel_id=1, source_target_pairs={{0,8},{2,10},{4,12},{6,14},{8,0},{10,2},{12,4},{14,6},{16,24},{18,... | collective-permute-start | bytes 417800 | tf_op jit(solution)/shard_map/ppermute | solution.py:31
  14.8 13.0 %collective-permute-start.4 = (bf16[272,256]{1,0:T(8,128)(2,1)S(1)}, bf16[272,256]{1,0:T(8,128)(2,1)S(1)}, u32[]{:S(2)}, u32[]{:S(2)}) collective-permute-start(bf16[272,256]{1,0:T(8,128)(2,1)S(1)} %pad_maximum_fusion.refs_0_), channel_id=1, source_target_pairs={{0,16},{2,18},{4,20},{6,22},{8,24},{10,26},{12,28},{14,30},{16,0},... | collective-permute-start | bytes 417800 | tf_op jit(solution)/shard_map/ppermute | solution.py:31
  17.5 10.4 %collective-permute-start.5 = (bf16[272,256]{1,0:T(8,128)(2,1)S(1)}, bf16[272,256]{1,0:T(8,128)(2,1)S(1)}, u32[]{:S(2)}, u32[]{:S(2)}) collective-permute-start(bf16[272,256]{1,0:T(8,128)(2,1)S(1)} %pad_maximum_fusion.refs_0_), channel_id=1, source_target_pairs={{0,24},{2,26},{4,28},{6,30},{8,16},{10,18},{12,20},{14,22},{16,8},... | collective-permute-start | bytes 417800 | tf_op jit(solution)/shard_map/ppermute | solution.py:31
  17.6 10.3 %collective-permute-start.6 = (bf16[272,256]{1,0:T(8,128)(2,1)S(1)}, bf16[272,256]{1,0:T(8,128)(2,1)S(1)}, u32[]{:S(2)}, u32[]{:S(2)}) collective-permute-start(bf16[272,256]{1,0:T(8,128)(2,1)S(1)} %pad_maximum_fusion.refs_0_), channel_id=1, source_target_pairs={{0,4},{2,6},{4,0},{6,2},{8,12},{10,14},{12,8},{14,10},{16,20},{18,... | collective-permute-start | bytes 417800 | tf_op jit(solution)/shard_map/ppermute | solution.py:31
  19.7 15.0 %copy-start.7 = (bf16[272,256]{1,0:T(8,128)(2,1)}, bf16[272,256]{1,0:T(8,128)(2,1)S(1)}, u32[]{:S(2)}) copy-start(bf16[272,256]{1,0:T(8,128)(2,1)S(1)} %collective-permute-done.3.refs_1_) | copy-start | bytes 417796
  19.7 8.1 %collective-permute-start.7 = (bf16[272,256]{1,0:T(8,128)(2,1)S(1)}, bf16[272,256]{1,0:T(8,128)(2,1)S(1)}, u32[]{:S(2)}, u32[]{:S(2)}) collective-permute-start(bf16[272,256]{1,0:T(8,128)(2,1)S(1)} %collective-permute-done.3.refs_1_), channel_id=1, source_target_pairs={{0,4},{2,6},{4,0},{6,2},{8,12},{10,14},{12,8},{14,10},{16,20},{18,... | collective-permute-start | bytes 417800 | tf_op jit(solution)/shard_map/ppermute | solution.py:31
  28.9 6.2 %collective-permute-start.10 = (bf16[272,256]{1,0:T(8,128)(2,1)S(1)}, bf16[272,256]{1,0:T(8,128)(2,1)S(1)}, u32[]{:S(2)}, u32[]{:S(2)}) collective-permute-start(bf16[272,256]{1,0:T(8,128)(2,1)S(1)} %pad_maximum_fusion.refs_0_), channel_id=1, source_target_pairs={{0,2},{2,0},{4,6},{6,4},{8,10},{10,8},{12,14},{14,12},{16,18},{18,... | collective-permute-start | bytes 417800 | tf_op jit(solution)/shard_map/ppermute | solution.py:31
  28.9 6.7 %collective-permute-start.11 = (bf16[272,256]{1,0:T(8,128)(2,1)S(1)}, bf16[272,256]{1,0:T(8,128)(2,1)}, u32[]{:S(2)}, u32[]{:S(2)}) collective-permute-start(bf16[272,256]{1,0:T(8,128)(2,1)S(1)} %collective-permute-done.3.refs_1_), channel_id=1, source_target_pairs={{0,2},{2,0},{4,6},{6,4},{8,10},{10,8},{12,14},{14,12},{16,18},{18,... | collective-permute-start | bytes 417800 | tf_op jit(solution)/shard_map/ppermute | solution.py:31
  29.4 7.9 %collective-permute-start.8 = (bf16[272,256]{1,0:T(8,128)(2,1)S(1)}, bf16[272,256]{1,0:T(8,128)(2,1)}, u32[]{:S(2)}, u32[]{:S(2)}) collective-permute-start(bf16[272,256]{1,0:T(8,128)(2,1)S(1)} %collective-permute-done.4.refs_0_), channel_id=1, source_target_pairs={{0,4},{2,6},{4,0},{6,2},{8,12},{10,14},{12,8},{14,10},{16,20},{18,... | collective-permute-start | bytes 417800 | tf_op jit(solution)/shard_map/ppermute | solution.py:31
  30.9 7.3 %collective-permute-start.9 = (bf16[272,256]{1,0:T(8,128)(2,1)S(1)}, bf16[272,256]{1,0:T(8,128)(2,1)}, u32[]{:S(2)}, u32[]{:S(2)}) collective-permute-start(bf16[272,256]{1,0:T(8,128)(2,1)S(1)} %collective-permute-done.5.refs_1_), channel_id=1, source_target_pairs={{0,4},{2,6},{4,0},{6,2},{8,12},{10,14},{12,8},{14,10},{16,20},{18,... | collective-permute-start | bytes 417800 | tf_op jit(solution)/shard_map/ppermute | solution.py:31
  31.5 7.2 %collective-permute-start.16 = (bf16[272,256]{1,0:T(8,128)(2,1)S(1)}, bf16[272,256]{1,0:T(8,128)(2,1)}, u32[]{:S(2)}, u32[]{:S(2)}) collective-permute-start(bf16[272,256]{1,0:T(8,128)(2,1)S(1)} %collective-permute-done.4.refs_0_), channel_id=1, source_target_pairs={{0,2},{2,0},{4,6},{6,4},{8,10},{10,8},{12,14},{14,12},{16,18},{18,... | collective-permute-start | bytes 417800 | tf_op jit(solution)/shard_map/ppermute | solution.py:31
  35.1 5.0 %collective-permute-start.17 = (bf16[272,256]{1,0:T(8,128)(2,1)S(1)}, bf16[272,256]{1,0:T(8,128)(2,1)S(1)}, u32[]{:S(2)}, u32[]{:S(2)}) collective-permute-start(bf16[272,256]{1,0:T(8,128)(2,1)S(1)} %collective-permute-done.5.refs_1_), channel_id=1, source_target_pairs={{0,2},{2,0},{4,6},{6,4},{8,10},{10,8},{12,14},{14,12},{16,18},{18,... | collective-permute-start | bytes 417800 | tf_op jit(solution)/shard_map/ppermute | solution.py:31
  38.2 4.4 %collective-permute-start.14 = (bf16[272,256]{1,0:T(8,128)(2,1)S(1)}, bf16[272,256]{1,0:T(8,128)(2,1)S(1)}, u32[]{:S(2)}, u32[]{:S(2)}) collective-permute-start(bf16[272,256]{1,0:T(8,128)(2,1)S(1)} %collective-permute-done.6.refs_0_), channel_id=1, source_target_pairs={{0,2},{2,0},{4,6},{6,4},{8,10},{10,8},{12,14},{14,12},{16,18},{18,... | collective-permute-start | bytes 417800 | tf_op jit(solution)/shard_map/ppermute | solution.py:31
  38.2 4.4 %collective-permute-start.15 = (bf16[272,256]{1,0:T(8,128)(2,1)S(1)}, bf16[272,256]{1,0:T(8,128)(2,1)S(1)}, u32[]{:S(2)}, u32[]{:S(2)}) collective-permute-start(bf16[272,256]{1,0:T(8,128)(2,1)S(1)} %collective-permute-done.7.refs_1_), channel_id=1, source_target_pairs={{0,2},{2,0},{4,6},{6,4},{8,10},{10,8},{12,14},{14,12},{16,18},{18,... | collective-permute-start | bytes 417800 | tf_op jit(solution)/shard_map/ppermute | solution.py:31
  38.7 6.4 %collective-permute-start.12 = (bf16[272,256]{1,0:T(8,128)(2,1)}, bf16[272,256]{1,0:T(8,128)(2,1)S(1)}, u32[]{:S(2)}, u32[]{:S(2)}) collective-permute-start(bf16[272,256]{1,0:T(8,128)(2,1)} %collective-permute-done.8.refs_0_), channel_id=1, source_target_pairs={{0,2},{2,0},{4,6},{6,4},{8,10},{10,8},{12,14},{14,12},{16,18},{18,... | collective-permute-start | bytes 417800 | tf_op jit(solution)/shard_map/ppermute | solution.py:31
  38.7 6.4 %collective-permute-start.13 = (bf16[272,256]{1,0:T(8,128)(2,1)}, bf16[272,256]{1,0:T(8,128)(2,1)S(1)}, u32[]{:S(2)}, u32[]{:S(2)}) collective-permute-start(bf16[272,256]{1,0:T(8,128)(2,1)} %collective-permute-done.9.refs_1_), channel_id=1, source_target_pairs={{0,2},{2,0},{4,6},{6,4},{8,10},{10,8},{12,14},{14,12},{16,18},{18,... | collective-permute-start | bytes 417800 | tf_op jit(solution)/shard_map/ppermute | solution.py:31
  45.9 3.7 %collective-permute-start.18 = (f32[2,1024]{1,0:T(2,128)S(1)}, f32[2,1024]{1,0:T(2,128)S(1)}, u32[]{:S(2)}, u32[]{:S(2)}) collective-permute-start(f32[2,1024]{1,0:T(2,128)S(1)} %shard_map.143.refs_0_), channel_id=1, source_target_pairs={{0,1},{1,0},{2,3},{3,2},{4,5},{5,4},{6,7},{7,6},{8,9},{9,8},{10,11... | collective-permute-start | bytes 24584 | tf_op jit(solution)/shard_map/ppermute | solution.py:31
  51.2 2.5 %collective-permute-start.21 = (f32[256,256]{1,0:T(8,128)S(1)}, f32[256,256]{1,0:T(8,128)S(1)}, u32[]{:S(2)}, u32[]{:S(2)}) collective-permute-start(f32[256,256]{1,0:T(8,128)S(1)} %get-tuple-element.157), channel_id=1, source_target_pairs={{0,2},{2,0},{4,6},{6,4},{8,10},{10,8},{12,14},{14,12},{16,18},{18,... | collective-permute-start | bytes 786440 | tf_op jit(solution)/shard_map/ppermute | solution.py:31
  51.3 2.4 %collective-permute-start.22 = (f32[256,256]{1,0:T(8,128)S(1)}, f32[256,256]{1,0:T(8,128)S(1)}, u32[]{:S(2)}, u32[]{:S(2)}) collective-permute-start(f32[256,256]{1,0:T(8,128)S(1)} %get-tuple-element.158), channel_id=1, source_target_pairs={{0,2},{2,0},{4,6},{6,4},{8,10},{10,8},{12,14},{14,12},{16,18},{18,... | collective-permute-start | bytes 786440 | tf_op jit(solution)/shard_map/ppermute | solution.py:31
  53.2 4.5 %collective-permute-start.19 = (f32[256,256]{1,0:T(8,128)S(1)}, f32[256,256]{1,0:T(8,128)S(1)}, u32[]{:S(2)}, u32[]{:S(2)}) collective-permute-start(f32[256,256]{1,0:T(8,128)S(1)} %get-tuple-element.155), channel_id=1, source_target_pairs={{0,2},{2,0},{4,6},{6,4},{8,10},{10,8},{12,14},{14,12},{16,18},{18,... | collective-permute-start | bytes 786440 | tf_op jit(solution)/shard_map/ppermute | solution.py:31
  53.3 4.4 %collective-permute-start.20 = (f32[256,256]{1,0:T(8,128)S(1)}, f32[256,256]{1,0:T(8,128)S(1)}, u32[]{:S(2)}, u32[]{:S(2)}) collective-permute-start(f32[256,256]{1,0:T(8,128)S(1)} %get-tuple-element.156), channel_id=1, source_target_pairs={{0,2},{2,0},{4,6},{6,4},{8,10},{10,8},{12,14},{14,12},{16,18},{18,... | collective-permute-start | bytes 786440 | tf_op jit(solution)/shard_map/ppermute | solution.py:31
  56.1 8.7 %collective-permute-start.28 = (f16[512,256]{1,0:T(8,128)(2,1)S(1)}, f16[512,256]{1,0:T(8,128)(2,1)S(1)}, u32[]{:S(2)}, u32[]{:S(2)}) collective-permute-start(f16[512,256]{1,0:T(8,128)(2,1)S(1)} %fusion.12), channel_id=1, source_target_pairs={{0,4},{2,6},{4,0},{6,2},{8,12},{10,14},{12,8},{14,10},{16,20},{18,... | collective-permute-start | bytes 786440 | tf_op jit(solution)/shard_map/ppermute | solution.py:31
  61.4 3.9 %collective-permute-start.26 = (f32[256,256]{1,0:T(8,128)S(1)}, f32[256,256]{1,0:T(8,128)S(1)}, u32[]{:S(2)}, u32[]{:S(2)}) collective-permute-start(f32[256,256]{1,0:T(8,128)S(1)} %get-tuple-element.177), channel_id=1, source_target_pairs={{0,2},{2,0},{4,6},{6,4},{8,10},{10,8},{12,14},{14,12},{16,18},{18,... | collective-permute-start | bytes 786440 | tf_op jit(solution)/shard_map/ppermute | solution.py:31
  61.5 5.1 %collective-permute-start.27 = (f32[256,256]{1,0:T(8,128)S(1)}, f32[256,256]{1,0:T(8,128)S(1)}, u32[]{:S(2)}, u32[]{:S(2)}) collective-permute-start(f32[256,256]{1,0:T(8,128)S(1)} %get-tuple-element.178), channel_id=1, source_target_pairs={{0,2},{2,0},{4,6},{6,4},{8,10},{10,8},{12,14},{14,12},{16,18},{18,... | collective-permute-start | bytes 786440 | tf_op jit(solution)/shard_map/ppermute | solution.py:31
  62.0 8.6 %collective-permute-start.25 = (f16[512,256]{1,0:T(8,128)(2,1)S(1)}, f16[512,256]{1,0:T(8,128)(2,1)S(1)}, u32[]{:S(2)}, u32[]{:S(2)}) collective-permute-start(f16[512,256]{1,0:T(8,128)(2,1)S(1)} %fusion.13), channel_id=1, source_target_pairs={{0,4},{2,6},{4,0},{6,2},{8,12},{10,14},{12,8},{14,10},{16,20},{18,... | collective-permute-start | bytes 786440 | tf_op jit(solution)/shard_map/ppermute | solution.py:31
  64.7 8.6 %collective-permute-start.23 = (f32[256,256]{1,0:T(8,128)S(1)}, f32[256,256]{1,0:T(8,128)S(1)}, u32[]{:S(2)}, u32[]{:S(2)}) collective-permute-start(f32[256,256]{1,0:T(8,128)S(1)} %get-tuple-element.174), channel_id=1, source_target_pairs={{0,2},{2,0},{4,6},{6,4},{8,10},{10,8},{12,14},{14,12},{16,18},{18,... | collective-permute-start | bytes 786440 | tf_op jit(solution)/shard_map/ppermute | solution.py:31
  64.8 8.5 %collective-permute-start.24 = (f32[256,256]{1,0:T(8,128)S(1)}, f32[256,256]{1,0:T(8,128)S(1)}, u32[]{:S(2)}, u32[]{:S(2)}) collective-permute-start(f32[256,256]{1,0:T(8,128)S(1)} %get-tuple-element.175), channel_id=1, source_target_pairs={{0,2},{2,0},{4,6},{6,4},{8,10},{10,8},{12,14},{14,12},{16,18},{18,... | collective-permute-start | bytes 786440 | tf_op jit(solution)/shard_map/ppermute | solution.py:31
  65.3 18.0 %collective-permute-start.32 = (bf16[256,768]{1,0:T(8,128)(2,1)S(1)}, bf16[256,768]{1,0:T(8,128)(2,1)S(1)}, u32[]{:S(2)}, u32[]{:S(2)}) collective-permute-start(bf16[256,768]{1,0:T(8,128)(2,1)S(1)} %copy-done.22), channel_id=1, source_target_pairs={{0,1},{1,0},{2,3},{3,2},{4,5},{5,4},{6,7},{7,6},{8,9},{9,8},{10,11... | collective-permute-start | bytes 1179656 | tf_op jit(solution)/shard_map/ppermute | solution.py:31
  68.0 8.1 %collective-permute-start.29 = (f16[256,256]{1,0:T(8,128)(2,1)S(1)}, f16[256,256]{1,0:T(8,128)(2,1)S(1)}, u32[]{:S(2)}, u32[]{:S(2)}) collective-permute-start(f16[256,256]{1,0:T(8,128)(2,1)S(1)} %get-tuple-element.246), channel_id=1, source_target_pairs={{0,24},{2,26},{4,28},{6,30},{8,16},{10,18},{12,20},{14,22},{16,8},... | collective-permute-start | bytes 393224 | tf_op jit(solution)/shard_map/ppermute | solution.py:31
  70.5 12.6 %collective-permute-start.30 = (f16[256,256]{1,0:T(8,128)(2,1)S(1)}, f16[256,256]{1,0:T(8,128)(2,1)S(1)}, u32[]{:S(2)}, u32[]{:S(2)}) collective-permute-start(f16[256,256]{1,0:T(8,128)(2,1)S(1)} %get-tuple-element.247), channel_id=1, source_target_pairs={{0,16},{2,18},{4,20},{6,22},{8,24},{10,26},{12,28},{14,30},{16,0},... | collective-permute-start | bytes 393224 | tf_op jit(solution)/shard_map/ppermute | solution.py:31
  74.8 8.4 %collective-permute-start.31 = (f16[256,256]{1,0:T(8,128)(2,1)S(1)}, f16[256,256]{1,0:T(8,128)(2,1)S(1)}, u32[]{:S(2)}, u32[]{:S(2)}) collective-permute-start(f16[256,256]{1,0:T(8,128)(2,1)S(1)} %multiply_convert_fusion.1), channel_id=1, source_target_pairs={{0,8},{2,10},{4,12},{6,14},{8,0},{10,2},{12,4},{14,6},{16,24},{18,... | collective-permute-start | bytes 393224 | tf_op jit(solution)/shard_map/ppermute | solution.py:31
  74.8 8.4 %collective-permute-start.33 = (f32[1,512]{1,0:T(1,128)S(1)}, f32[1,512]{1,0:T(1,128)S(1)}, u32[]{:S(2)}, u32[]{:S(2)}) collective-permute-start(f32[1,512]{1,0:T(1,128)S(1)} %bitcast.113), channel_id=1, source_target_pairs={{0,1},{1,0},{2,3},{3,2},{4,5},{5,4},{6,7},{7,6},{8,9},{9,8},{10,11... | collective-permute-start | bytes 6152 | tf_op jit(solution)/shard_map/ppermute | solution.py:31
  83.3 1.8 %collective-permute-start.35 = (bf16[256,768]{1,0:T(8,128)(2,1)S(1)}, bf16[256,768]{1,0:T(8,128)(2,1)S(1)}, u32[]{:S(2)}, u32[]{:S(2)}) collective-permute-start(bf16[256,768]{1,0:T(8,128)(2,1)S(1)} %collective-permute-done.32), channel_id=1, source_target_pairs={{0,2},{2,0},{4,6},{6,4},{8,10},{10,8},{12,14},{14,12},{16,18},{18,... | collective-permute-start | bytes 1179656 | tf_op jit(solution)/shard_map/ppermute | solution.py:31
  83.5 5.9 %collective-permute-start.34 = (bf16[256,256]{1,0:T(8,128)(2,1)S(1)}, bf16[256,256]{1,0:T(8,128)(2,1)S(1)}, u32[]{:S(2)}, u32[]{:S(2)}) collective-permute-start(bf16[256,256]{1,0:T(8,128)(2,1)S(1)} %add_convert_fusion.1.refs_0_), channel_id=1, source_target_pairs={{0,1},{1,0},{2,3},{3,2},{4,5},{5,4},{6,7},{7,6},{8,9},{9,8},{10,11... | collective-permute-start | bytes 393224 | tf_op jit(solution)/shard_map/ppermute | solution.py:31
  91.3 1.8 %collective-permute-start.36 = (f16[256,768]{1,0:T(8,128)(2,1)S(1)}, f16[256,768]{1,0:T(8,128)(2,1)S(1)}, u32[]{:S(2)}, u32[]{:S(2)}) collective-permute-start(f16[256,768]{1,0:T(8,128)(2,1)S(1)} %dynamic-slice_convert_fusion), channel_id=1, source_target_pairs={{0,2},{2,0},{4,6},{6,4},{8,10},{10,8},{12,14},{14,12},{16,18},{18,... | collective-permute-start | bytes 1179656 | tf_op jit(solution)/shard_map/ppermute | solution.py:31
  91.4 1.7 %collective-permute-start.37 = (f32[1,512]{1,0:T(1,128)S(1)}, f32[1,512]{1,0:T(1,128)S(1)}, u32[]{:S(2)}, u32[]{:S(2)}) collective-permute-start(f32[1,512]{1,0:T(1,128)S(1)} %get-tuple-element.207), channel_id=1, source_target_pairs={{0,2},{2,0},{4,6},{6,4},{8,10},{10,8},{12,14},{14,12},{16,18},{18,... | collective-permute-start | bytes 6152 | tf_op jit(solution)/shard_map/ppermute | solution.py:31
  94.0 5.8 %collective-permute-start.38 = (f32[1,512]{1,0:T(1,128)S(1)}, f32[1,512]{1,0:T(1,128)S(1)}, u32[]{:S(2)}, u32[]{:S(2)}) collective-permute-start(f32[1,512]{1,0:T(1,128)S(1)} %add.333), channel_id=1, source_target_pairs={{0,16},{2,18},{4,20},{6,22},{8,24},{10,26},{12,28},{14,30},{16,0},... | collective-permute-start | bytes 6152 | tf_op jit(solution)/shard_map/ppermute | solution.py:31
  94.0 17.5 %all-to-all-start = ((f16[8,32,768]{2,1,0:T(8,128)(2,1)}), f16[8,32,768]{2,1,0:T(8,128)(2,1)}, u32[]{:S(2)}, u32[]{:S(2)}) async-start(f16[8,32,768]{2,1,0:T(8,128)(2,1)} %bitcast.11), calls=%async_computation | async-start | bytes 786432 | tf_op jit(solution)/shard_map/all_to_all | solution.py:435
  99.8 6.7 %collective-permute-start.39 = (f32[1,512]{1,0:T(1,128)S(1)}, f32[1,512]{1,0:T(1,128)S(1)}, u32[]{:S(2)}, u32[]{:S(2)}) collective-permute-start(f32[1,512]{1,0:T(1,128)S(1)} %add.335), channel_id=1, source_target_pairs={{0,8},{2,10},{4,12},{6,14},{8,0},{10,2},{12,4},{14,6},{16,24},{18,... | collective-permute-start | bytes 6152 | tf_op jit(solution)/shard_map/ppermute | solution.py:31
  106.4 4.4 %collective-permute-start.40 = (f32[1,512]{1,0:T(1,128)S(1)}, f32[1,512]{1,0:T(1,128)S(1)}, u32[]{:S(2)}, u32[]{:S(2)}) collective-permute-start(f32[1,512]{1,0:T(1,128)S(1)} %add.336), channel_id=1, source_target_pairs={{0,4},{2,6},{4,0},{6,2},{8,12},{10,14},{12,8},{14,10},{16,20},{18,... | collective-permute-start | bytes 6152 | tf_op jit(solution)/shard_map/ppermute | solution.py:31
  113.4 15.7 %all-to-all-start.1 = ((f16[8,32,768]{2,1,0:T(8,128)(2,1)}), f16[8,32,768]{2,1,0:T(8,128)(2,1)S(1)}, u32[]{:S(2)}, u32[]{:S(2)}) async-start(f16[8,32,768]{2,1,0:T(8,128)(2,1)} %broadcast_in_dim.79), calls=%async_computation.1 | async-start | bytes 786432 | tf_op jit(solution)/shard_map/all_to_all | solution.py:435
  119.0 3.8 %collective-permute-start.41 = (f32[1,1024]{1,0:T(1,128)S(1)}, f32[1,1024]{1,0:T(1,128)S(1)}, u32[]{:S(2)}, u32[]{:S(2)}) collective-permute-start(f32[1,1024]{1,0:T(1,128)S(1)} %bitcast.99), channel_id=1, source_target_pairs={{0,1},{1,0},{2,3},{3,2},{4,5},{5,4},{6,7},{7,6},{8,9},{9,8},{10,11... | collective-permute-start | bytes 12296 | tf_op jit(solution)/shard_map/ppermute | solution.py:31
  120.2 6.4 %collective-permute-start.42 = (f16[256,512]{1,0:T(8,128)(2,1)S(1)}, f16[256,512]{1,0:T(8,128)(2,1)S(1)}, u32[]{:S(2)}, u32[]{:S(2)}) collective-permute-start(f16[256,512]{1,0:T(8,128)(2,1)S(1)} %multiply_convert_fusion), channel_id=1, source_target_pairs={{0,1},{1,0},{2,3},{3,2},{4,5},{5,4},{6,7},{7,6},{8,9},{9,8},{10,11... | collective-permute-start | bytes 786440 | tf_op jit(solution)/shard_map/ppermute | solution.py:31
  129.1 1.7 %collective-permute-start.43 = (f16[256,768]{1,0:T(8,128)(2,1)S(1)}, f16[256,768]{1,0:T(8,128)(2,1)S(1)}, u32[]{:S(2)}, u32[]{:S(2)}) collective-permute-start(f16[256,768]{1,0:T(8,128)(2,1)S(1)} %bitcast.96), channel_id=1, source_target_pairs={{0,2},{2,0},{4,6},{6,4},{8,10},{10,8},{12,14},{14,12},{16,18},{18,... | collective-permute-start | bytes 1179656 | tf_op jit(solution)/shard_map/ppermute | solution.py:31
  (27 other events, 175.3 us)
where the time goes:
time: 133 us
  starting transfers between devices  48.8 us (37%)
  waiting for transfers between devices  34.1 us (26%)
  Pallas kernels  24.3 us (18%)
  other arithmetic  10 us (8%)
  matrix products  9.06 us (7%)
  local copies, waits for them, and re-layouts  3.41 us (3%)
  between operations  3.13 us (2%)
    ppermute x44, starting transfers between devices, hop(): return lax.ppermute(value, axis, [(i, i ^ bits) for i in range(size)])  37.4 us
    ppermute x44, waiting for transfers between devices, hop(): return lax.ppermute(value, axis, [(i, i ^ bits) for i in range(size)])  32.7 us
    pallas_call x8, Pallas kernels, run_grad(): pl.pallas_call(functools.partial(grad_kernel, scale, base, count, len(mor...  13.6 us
    all_to_all x2, starting transfers between devices, exchange(): lax.all_to_all(blocks, 'dp', split_axis=0, concat_axis=0, axis_index_grou...  11.4 us
    dot_general x7, matrix products, dot(): return lax.dot_general(a, b, dims, preferred_element_type=F32, **kw)  9.06 us
    pallas_call x8, Pallas kernels, run_stats(): pl.pallas_call(functools.partial(stats_kernel, scale, base, count, last),...  8.87 us
  transfers between devices with their start and end apart: 46, of which 16 were waited for; matrix products, arithmetic and copies ran while one was open for 10% of the time, Pallas kernels for 15%

commit v1 on v0

--- a/solution.py
+++ b/solution.py
@@ -158,7 +158,7 @@
     return sums, qg, sp
 
 
-def backward_kernel(count, index_ref, factor_ref, *refs):
+def backward_kernel(count, index_ref, scale_ref, *refs):
     grad_refs, (pre_ref, hidden_ref, emb_ref, w_out_ref) = refs[:count], refs[count : count + 4]
     grad_ref, pre_grad_ref, b_ref, *sums_refs = refs[count + 4 :]
     part = grad_refs[0].shape[0]
@@ -169,8 +169,8 @@
     pre_grad = jnp.where(pre_ref[...] > 0.0, back, 0.0).astype(BF16)
     pre_grad_ref[...] = pre_grad
     b_ref[...] = jnp.sum(pre_grad.astype(F32), axis=0, keepdims=True)
-    sums_in = dot(emb_ref[...], pre_grad, TN) * factor_ref[0]
-    sums_out = dot(hidden_ref[...], grad_ref[...], TN) * factor_ref[1]
+    sums_in = dot(emb_ref[...], pre_grad, TN) * scale_ref[2:3, : pre_grad.shape[1]]
+    sums_out = dot(hidden_ref[...], grad_ref[...], TN) * scale_ref[3:4, : grad_ref.shape[1]]
     if len(sums_refs) == 1:
         units = sums_in.shape[1]
         sums_refs[0][:, :units] = sums_in
@@ -180,7 +180,7 @@
         sums_refs[1][...] = sums_out
 
 
-def run_backward(index, factors, grads, pre, hidden, emb, w_out):
+def run_backward(index, scales, grads, pre, hidden, emb, w_out):
     rows, units = pre.shape
     width_emb, width_out = emb.shape[1], w_out.shape[1]
     if units == width_emb:
@@ -189,7 +189,7 @@
         sums = [(width_emb, units), (units, width_out)]
     grad, pre_grad, local_b, *sums = pl.pallas_call(
         functools.partial(backward_kernel, len(grads)),
-        in_specs=[pl.BlockSpec(memory_space=pltpu.SMEM)] * 2 + in_vmem(len(grads) + 4),
+        in_specs=[pl.BlockSpec(memory_space=pltpu.SMEM)] + in_vmem(len(grads) + 5),
         out_specs=in_vmem(3 + len(sums)),
         out_shape=[
             jax.ShapeDtypeStruct((rows, width_out), BF16),
@@ -198,10 +198,29 @@
         ]
         + [jax.ShapeDtypeStruct(shape, F32) for shape in sums],
         compiler_params=pltpu.CompilerParams(vmem_limit_bytes=12 << 20),
-    )(index, factors, *grads, pre, hidden, emb, w_out)
+    )(index, scales, *grads, pre, hidden, emb, w_out)
     if len(sums) > 1:
         sums = [jnp.concatenate([sums[0], sums[1].reshape(width_emb, -1)], axis=1)]
     return grad, pre_grad, local_b, sums[0]
+
+
+def scale_kernel(bounds, words_ref, scale_ref):
+    exponent = jnp.max(words_ref[...] >> WORD_BITS, axis=1, keepdims=True)
+    exponent = jnp.max(exponent, axis=0, keepdims=True) - EXPONENT_BASE
+    largest = jnp.exp2(jnp.broadcast_to(exponent.astype(F32), (1, scale_ref.shape[1])))
+    for n, bound in enumerate(bounds):
+        scale_ref[n : n + 1] = (LIMIT / bound) / largest
+        scale_ref[n + len(bounds) : n + len(bounds) + 1] = largest * (bound / LIMIT)
+
+
+def run_scale(bounds, words, width):
+    return pl.pallas_call(
+        functools.partial(scale_kernel, bounds),
+        in_specs=in_vmem(1),
+        out_specs=in_vmem(1)[0],
+        out_shape=jax.ShapeDtypeStruct((2 * len(bounds), width), F32),
+        compiler_params=pltpu.CompilerParams(vmem_limit_bytes=2 << 20),
+    )(words)
 
 
 def joined(mine, other, first):
@@ -265,7 +284,18 @@
     words = jnp.concatenate([word, hop(word, 1)], axis=0)
     words = jnp.concatenate([words, hop(words, 2)], axis=0)
 
-    total, arrived, qt, piece = tie((part_of(partial, 0), arrived, qt, piece))
+    total, arrived, qt, piece, share_starts, half_starts, model_index, core_first = tie(
+        (
+            part_of(partial, 0),
+            arrived,
+            qt,
+            piece,
+            share_starts,
+            half_starts,
+            model_index,
+            core_first,
+        )
+    )
     for other in arrived:
         total = total + other
     size = 4 * cand_local
@@ -286,7 +316,6 @@
 
     flat = words.reshape(-1)
     n_cand = flat.shape[0]
-    q_bound = jnp.exp2((jnp.max(flat >> WORD_BITS) - EXPONENT_BASE).astype(F32))
     flat = flat & ((1 << WORD_BITS) - 1)
 
     hidden_max = width_emb * TABLE_MAX * W_IN_MAX + B_IN_MAX
@@ -297,8 +326,9 @@
         gradient_sum * width_out * W_OUT_MAX * TABLE_MAX,
         gradient_sum * hidden_max,
     ]
-    factors = [(LIMIT / bound) / q_bound for bound in bounds]
-    growths = [q_bound * (bound / LIMIT) for bound in bounds]
+    scales = run_scale(bounds, words, max(units, width_out))
+    factors = [scales[n : n + 1] for n in range(4)]
+    growths = [scales[n + 4 : n + 5] for n in range(4)]
     row = (flat // COUNT_BASE) % rows
     column = place((flat // (COUNT_BASE * rows)) ^ me) * part + row % part
     column = jnp.where(row // part == my_model, column, -1)
@@ -309,9 +339,7 @@
     weight = dot(low, high, NT, precision=lax.Precision.HIGHEST)
     bias = jnp.where(weight > 0.0, jnp.log2(weight), ABSENT)
     own_mask = dot(item_table, packed[:, :units]) + b_in[None, :] > 0.0
-    bias, factors, growths, share_starts, half_starts, model_index, core_first, own_mask = tie(
-        (bias, factors, growths, share_starts, half_starts, model_index, core_first, own_mask)
-    )
+    bias, own_mask = tie((bias, own_mask))
 
     spot = ((positive // cand_local) ^ me) * cand_local + positive % cand_local
     side = 64
@@ -380,7 +408,7 @@
     for h in (1, 0):
         chip_sums[1, h], qg, sp = gradients((1, 0, h), qg, sp, siblings[1, h])
         crossing[h], qg = tie(
-            ((jnp.concatenate(chip_sums[1, h], axis=0) * factors[0]).astype(F16), qg)
+            ((jnp.concatenate(chip_sums[1, h], axis=0) * factors[0][:, :width_out]).astype(F16), qg)
         )
         crossed[h] = hop(crossing[h], 2)
     for h in (1, 0):
@@ -390,12 +418,12 @@
         crossed[h], qg = tie((crossed[h], qg))
         chip_sums[0, h], qg, sp = gradients((0, 0, h), qg, sp, siblings[0, h])
         for j in range(n_z // 2):
-            over = crossed[h][j * part : (j + 1) * part].astype(F32) * growths[0]
+            over = crossed[h][j * part : (j + 1) * part].astype(F32) * growths[0][:, :width_out]
             z_sums[h * n_z // 2 + j] = chip_sums[0, h][j] + over
     own_sum = z_sums[0]
     for j in range(n_z - 1, 0, -1):
-        sent = hop((z_sums[j] * factors[1]).astype(F16), j << 2)
-        own_sum = own_sum + sent.astype(F32) * growths[1]
+        sent = hop((z_sums[j] * factors[1][:, :width_out]).astype(F16), j << 2)
+        own_sum = own_sum + sent.astype(F32) * growths[1][:, :width_out]
     own_grad, others = tie((own_sum.astype(BF16), others))
     others = [(joined(got, hop(got, 1), core_first), b) for got, b in others]
     weights = [(packed, b_in[None, :])] + others
@@ -412,7 +440,7 @@
     grads = [own_grad] + [hop(own_grad, k, "mp") for k in range(1, n_model)]
     grads, masks = tie((grads, masks))
     item_grad, pre_grad, local_b, value = run_backward(
-        model_index, jnp.stack(factors[2:]), grads, pre, hidden, item_table, w_out
+        model_index, scales, grads, pre, hidden, item_table, w_out
     )
 
     width = value.shape[1]
@@ -446,9 +474,10 @@
     pieces = exchange(value.reshape(chips, size, width))
     pieces, grad_table = tie((pieces, grad_table))
     total = jnp.sum(pieces.astype(F32), axis=0).astype(F16)
-    total, local_b = tie((total, step_bias(local_b, 9)))
+    total, local_b = tie((total, step_bias(local_b, 2)))
     own_half = exchange(jnp.broadcast_to(total[None], (chips, size, width)))
     own_half = own_half.reshape(half_rows, width)
+    local_b = step_bias(local_b, 9)
 
     local_b, qg, sp = tie((local_b, qg, sp))
 
@@ -468,8 +497,9 @@
     query_grad = (query_sum * scale).T
 
     sides = [own_half, hop(own_half, 1)]
-    sides_in = [v[:, :units].astype(F32) * growths[2] for v in sides]
-    sides_out = [v[:, units:].astype(F32) * growths[3] for v in sides]
+    sides_in = [v[:, :units].astype(F32) * growths[2][:, :units] for v in sides]
+    tail_width = width - units
+    sides_out = [v[:, units:].astype(F32) * growths[3][:, :tail_width] for v in sides]
     grad_w_in = joined(*sides_in, core_first)
     grad_w_out = joined(*sides_out, core_first).reshape(units, width_out)
     return (loss, query_grad, grad_w_in, local_b[0], grad_w_out, grad_table)

time: 133 us -> 140 us (1.053)
  waiting for transfers between devices: 34.1 us -> 44.5 us
  starting transfers between devices: 48.8 us -> 46.7 us
    ppermute x44, waiting for transfers between devices: 32.7 us -> 42.6 us  [hop(): return lax.ppermute(value, axis, [(i, i ^ bits) for i in range(size)])]
    all_to_all x2, starting transfers between devices: 11.4 us -> 8.44 us  [exchange(): lax.all_to_all(blocks, 'dp', split_axis=0, concat_axis=0, axis_index_grou...]
  transfers between devices with their start and end apart: 46 -> 46, of which waited for: 16 -> 18; matrix products, arithmetic and copies ran while one was open for 10% -> 10% of each run, Pallas kernels for 15% -> 15%
where the time goes in v1:
time: 140 us; the launch traced here: 139 us
  starting transfers between devices  46.7 us (33%)
  waiting for transfers between devices  44.5 us (32%)
  Pallas kernels  23.8 us (17%)
  other arithmetic  9.53 us (7%)
  matrix products  9.06 us (6%)
  local copies, waits for them, and re-layouts  3.42 us (2%)
  between operations  2.26 us (2%)
    ppermute x44, waiting for transfers between devices, hop(): return lax.ppermute(value, axis, [(i, i ^ bits) for i in range(size)])  42.6 us
    ppermute x44, starting transfers between devices, hop(): return lax.ppermute(value, axis, [(i, i ^ bits) for i in range(size)])  38.3 us
    pallas_call x8, Pallas kernels, run_grad(): pl.pallas_call(functools.partial(grad_kernel, scale, base, count, len(mor...  13.4 us
    dot_general x7, matrix products, dot(): return lax.dot_general(a, b, dims, preferred_element_type=F32, **kw)  9.06 us
    pallas_call x8, Pallas kernels, run_stats(): pl.pallas_call(functools.partial(stats_kernel, scale, base, count, last),...  8.88 us
    all_to_all x2, starting transfers between devices, exchange(): lax.all_to_all(blocks, 'dp', split_axis=0, concat_axis=0, axis_index_grou...  8.44 us
  transfers between devices with their start and end apart: 46, of which 18 were waited for; matrix products, arithmetic and copies ran while one was open for 10% of the time, Pallas kernels for 15%

profile of v1, /device:TPU:0, one launch (start us, length us, event | category | flops | bytes accessed | tf_op | source)
XLA Modules:
  0.0 139.3 jit_solution(13578078352880141470)
XLA Ops:
  0.6 1.7 %maximum_convert_fusion = (bf16[512,512]{1,0:T(8,128)(2,1)S(1)}, f32[512,512]{1,0:T(8,128)S(1)}) fusion(f32[512]{0:T(512)} %param.16, bf16[512,512]{1,0:T(8,128)(2,1)} %refs_4_.1, bf16[512,512]{1,0:T(8,128)(2,1)} %param.15), kind=kOutput, calls=%fused_computation.14 | convolution fusion | flops 269221888 | bytes 2623488 | tf_op jit(solution)/shard_map/dot_general | solution.py:37
  3.5 3.0 %collective-permute-start = (f32[256,256]{1,0:T(8,128)S(1)}, f32[256,256]{1,0:T(8,128)S(1)}, u32[]{:S(2)}, u32[]{:S(2)}) collective-permute-start(f32[256,256]{1,0:T(8,128)S(1)} %get-tuple-element.222), channel_id=1, source_target_pairs={{0,1},{1,0},{2,3},{3,2},{4,5},{5,4},{6,7},{7,6},{8,9},{9,8},{10,11... | collective-permute-start | bytes 786440 | tf_op jit(solution)/shard_map/ppermute | solution.py:31
  9.2 1.6 %collective-permute-start.2 = (s32[2,256]{1,0:T(2,128)S(1)}, s32[2,256]{1,0:T(2,128)S(1)}, u32[]{:S(2)}, u32[]{:S(2)}) collective-permute-start(s32[2,256]{1,0:T(2,128)S(1)} %pad_add_fusion.1), channel_id=1, source_target_pairs={{0,4},{2,6},{4,0},{6,2},{8,12},{10,14},{12,8},{14,10},{16,20},{18,... | collective-permute-start | bytes 6152 | tf_op jit(solution)/shard_map/ppermute | solution.py:31
  13.1 1.7 %collective-permute-start.3 = (bf16[272,256]{1,0:T(8,128)(2,1)S(1)}, bf16[272,256]{1,0:T(8,128)(2,1)S(1)}, u32[]{:S(2)}, u32[]{:S(2)}) collective-permute-start(bf16[272,256]{1,0:T(8,128)(2,1)S(1)} %pad_maximum_fusion.refs_0_), channel_id=1, source_target_pairs={{0,8},{2,10},{4,12},{6,14},{8,0},{10,2},{12,4},{14,6},{16,24},{18,... | collective-permute-start | bytes 417800 | tf_op jit(solution)/shard_map/ppermute | solution.py:31
  14.8 2.7 %collective-permute-start.4 = (bf16[272,256]{1,0:T(8,128)(2,1)S(1)}, bf16[272,256]{1,0:T(8,128)(2,1)S(1)}, u32[]{:S(2)}, u32[]{:S(2)}) collective-permute-start(bf16[272,256]{1,0:T(8,128)(2,1)S(1)} %pad_maximum_fusion.refs_0_), channel_id=1, source_target_pairs={{0,16},{2,18},{4,20},{6,22},{8,24},{10,26},{12,28},{14,30},{16,0},... | collective-permute-start | bytes 417800 | tf_op jit(solution)/shard_map/ppermute | solution.py:31
  17.6 1.6 %collective-permute-start.6 = (bf16[272,256]{1,0:T(8,128)(2,1)S(1)}, bf16[272,256]{1,0:T(8,128)(2,1)S(1)}, u32[]{:S(2)}, u32[]{:S(2)}) collective-permute-start(bf16[272,256]{1,0:T(8,128)(2,1)S(1)} %pad_maximum_fusion.refs_0_), channel_id=1, source_target_pairs={{0,4},{2,6},{4,0},{6,2},{8,12},{10,14},{12,8},{14,10},{16,20},{18,... | collective-permute-start | bytes 417800 | tf_op jit(solution)/shard_map/ppermute | solution.py:31
  19.7 1.6 %collective-permute-start.7 = (bf16[272,256]{1,0:T(8,128)(2,1)S(1)}, bf16[272,256]{1,0:T(8,128)(2,1)S(1)}, u32[]{:S(2)}, u32[]{:S(2)}) collective-permute-start(bf16[272,256]{1,0:T(8,128)(2,1)S(1)} %collective-permute-done.3.refs_1_), channel_id=1, source_target_pairs={{0,4},{2,6},{4,0},{6,2},{8,12},{10,14},{12,8},{14,10},{16,20},{18,... | collective-permute-start | bytes 417800 | tf_op jit(solution)/shard_map/ppermute | solution.py:31
  21.4 6.5 %collective-permute-done.4.refs_0_ = bf16[272,256]{1,0:T(8,128)(2,1)S(1)} collective-permute-done((bf16[272,256]{1,0:T(8,128)(2,1)S(1)}, bf16[272,256]{1,0:T(8,128)(2,1)S(1)}, u32[]{:S(2)}, u32[]{:S(2)}) %collective-permute-start.4) | collective-permute-done | bytes 139296 | tf_op jit(solution)/shard_map/ppermute | solution.py:31
  28.8 1.5 %collective-permute-start.8 = (bf16[272,256]{1,0:T(8,128)(2,1)S(1)}, bf16[272,256]{1,0:T(8,128)(2,1)}, u32[]{:S(2)}, u32[]{:S(2)}) collective-permute-start(bf16[272,256]{1,0:T(8,128)(2,1)S(1)} %collective-permute-done.4.refs_0_), channel_id=1, source_target_pairs={{0,4},{2,6},{4,0},{6,2},{8,12},{10,14},{12,8},{14,10},{16,20},{18,... | collective-permute-start | bytes 417800 | tf_op jit(solution)/shard_map/ppermute | solution.py:31
  31.1 1.3 multiply_select_fusion.refs_3_.refs_4_.refs_6_
  34.2 1.7 %shard_map.137 = (f32[8,1024]{1,0:T(8,128)S(1)}, f32[8,1024]{1,0:T(8,128)S(1)}) custom-call(bf16[272,256]{1,0:T(8,128)(2,1)S(1)} %collective-permute-done.10.refs_0_, bf16[272,256]{1,0:T(8,128)(2,1)} %collective-permute-done.11.refs_1_, bf16[256,1024]{1,0:T(8,128)(2,1)S(1)} %bitcast.85, f32[128,32]{1,0:T(8,128)S(1)} %multiply_select_fusion.refs_3_.refs_4_.refs_6_, ...), custom_call_target="tpu_custom_call" | custom-call | tf_op jit(solution)/shard_map/pallas_call | solution.py:80
  35.9 1.7 %collective-permute-done.9.refs_1_ = bf16[272,256]{1,0:T(8,128)(2,1)} collective-permute-done((bf16[272,256]{1,0:T(8,128)(2,1)S(1)}, bf16[272,256]{1,0:T(8,128)(2,1)}, u32[]{:S(2)}, u32[]{:S(2)}) %collective-permute-start.9) | collective-permute-done | bytes 139296 | tf_op jit(solution)/shard_map/ppermute | solution.py:31
  39.5 1.7 %shard_map.139 = (f32[8,1024]{1,0:T(8,128)S(1)}, f32[8,1024]{1,0:T(8,128)S(1)}) custom-call(bf16[272,256]{1,0:T(8,128)(2,1)} %collective-permute-done.16.refs_0_, bf16[272,256]{1,0:T(8,128)(2,1)S(1)} %collective-permute-done.17.refs_1_, bf16[256,1024]{1,0:T(8,128)(2,1)S(1)} %bitcast.87, f32[128,32]{1,0:T(8,128)S(1)} %multiply_select_fusion.refs_3_.refs_4_.refs_6_, ...), custom_call_target="tpu_custom_call" | custom-call | tf_op jit(solution)/shard_map/pallas_call | solution.py:80
  42.7 1.7 %shard_map.142 = (f32[8,1024]{1,0:T(8,128)S(1)}, f32[8,1024]{1,0:T(8,128)S(1)}) custom-call(bf16[272,256]{1,0:T(8,128)(2,1)} %collective-permute-done.8.refs_0_, bf16[272,256]{1,0:T(8,128)(2,1)} %collective-permute-done.9.refs_1_, bf16[256,1024]{1,0:T(8,128)(2,1)S(1)} %bitcast.90, f32[128,32]{1,0:T(8,128)S(1)} %multiply_select_fusion.refs_3_.refs_4_.refs_6_, ...), custom_call_target="tpu_custom_call" | custom-call | tf_op jit(solution)/shard_map/pallas_call | solution.py:80
  45.3 1.3 collective-permute-start.18
  46.6 2.3 %collective-permute-done.18.refs_1_ = f32[2,1024]{1,0:T(2,128)S(1)} collective-permute-done((f32[2,1024]{1,0:T(2,128)S(1)}, f32[2,1024]{1,0:T(2,128)S(1)}, u32[]{:S(2)}, u32[]{:S(2)}) %collective-permute-start.18) | collective-permute-done | bytes 8224 | tf_op jit(solution)/shard_map/ppermute | solution.py:31
  49.1 1.3 shard_map.146
  51.4 1.3 shard_map.147
  53.4 2.3 %shard_map.148 = (f32[256,256]{1,0:T(8,128)S(1)}, f32[256,256]{1,0:T(8,128)S(1)}, f32[256,1024]{1,0:T(8,128)S(1)}, f32[8,1024]{1,0:T(8,128)S(1)}) custom-call(bf16[272,256]{1,0:T(8,128)(2,1)} %collective-permute-done.8.refs_0_, bf16[272,256]{1,0:T(8,128)(2,1)} %collective-permute-done.9.refs_1_, ...), custom_call_target="tpu_custom_call", output_to_operand_aliasing={{2}: (9, {}), {3}: (10, {})} | custom-call | tf_op jit(solution)/shard_map/pallas_call | solution.py:147
  55.8 1.6 %collective-permute-start.28 = (f16[512,256]{1,0:T(8,128)(2,1)S(1)}, f16[512,256]{1,0:T(8,128)(2,1)S(1)}, u32[]{:S(2)}, u32[]{:S(2)}) collective-permute-start(f16[512,256]{1,0:T(8,128)(2,1)S(1)} %fusion.12), channel_id=1, source_target_pairs={{0,4},{2,6},{4,0},{6,2},{8,12},{10,14},{12,8},{14,10},{16,20},{18,... | collective-permute-start | bytes 786440 | tf_op jit(solution)/shard_map/ppermute | solution.py:31
  57.3 1.3 shard_map.149
  58.7 2.2 %shard_map.150 = (f32[256,256]{1,0:T(8,128)S(1)}, f32[256,256]{1,0:T(8,128)S(1)}, f32[256,1024]{1,0:T(8,128)S(1)}, f32[8,1024]{1,0:T(8,128)S(1)}) custom-call(bf16[272,256]{1,0:T(8,128)(2,1)} %collective-permute-done.16.refs_0_, bf16[272,256]{1,0:T(8,128)(2,1)S(1)} %collective-permute-done.17.refs_1_, ...), custom_call_target="tpu_custom_call", output_to_operand_aliasing={{2}: (7, {}), {3}: (8, {})} | custom-call | tf_op jit(solution)/shard_map/pallas_call | solution.py:147
  62.1 2.2 %shard_map.151 = (f32[256,256]{1,0:T(8,128)S(1)}, f32[256,256]{1,0:T(8,128)S(1)}, f32[256,1024]{1,0:T(8,128)S(1)}, f32[8,1024]{1,0:T(8,128)S(1)}) custom-call(bf16[272,256]{1,0:T(8,128)(2,1)S(1)} %copy-done.18, bf16[272,256]{1,0:T(8,128)(2,1)} %collective-permute-done.11.refs_1_, ...), custom_call_target="tpu_custom_call", output_to_operand_aliasing={{2}: (7, {}), {3}: (8, {})} | custom-call | tf_op jit(solution)/shard_map/pallas_call | solution.py:147
  64.9 1.2 collective-permute-start.32
  66.1 1.3 shard_map.152
  67.5 2.4 %collective-permute-done.25 = f16[512,256]{1,0:T(8,128)(2,1)S(1)} collective-permute-done((f16[512,256]{1,0:T(8,128)(2,1)S(1)}, f16[512,256]{1,0:T(8,128)(2,1)S(1)}, u32[]{:S(2)}, u32[]{:S(2)}) %collective-permute-start.25) | collective-permute-done | bytes 262176 | tf_op jit(solution)/shard_map/ppermute | solution.py:31
  69.9 1.3 shard_map.153
  71.4 2.5 %collective-permute-start.29 = (f16[256,256]{1,0:T(8,128)(2,1)S(1)}, f16[256,256]{1,0:T(8,128)(2,1)S(1)}, u32[]{:S(2)}, u32[]{:S(2)}) collective-permute-start(f16[256,256]{1,0:T(8,128)(2,1)S(1)} %get-tuple-element.224), channel_id=1, source_target_pairs={{0,24},{2,26},{4,28},{6,30},{8,16},{10,18},{12,20},{14,22},{16,8},... | collective-permute-start | bytes 393224 | tf_op jit(solution)/shard_map/ppermute | solution.py:31
  75.9 1.2 collective-permute-start.33
  77.0 2.5 %collective-permute-done.29 = f16[256,256]{1,0:T(8,128)(2,1)S(1)} collective-permute-done((f16[256,256]{1,0:T(8,128)(2,1)S(1)}, f16[256,256]{1,0:T(8,128)(2,1)S(1)}, u32[]{:S(2)}, u32[]{:S(2)}) %collective-permute-start.29) | collective-permute-done | bytes 131104 | tf_op jit(solution)/shard_map/ppermute | solution.py:31
  79.5 6.5 %collective-permute-done.30 = f16[256,256]{1,0:T(8,128)(2,1)S(1)} collective-permute-done((f16[256,256]{1,0:T(8,128)(2,1)S(1)}, f16[256,256]{1,0:T(8,128)(2,1)S(1)}, u32[]{:S(2)}, u32[]{:S(2)}) %collective-permute-start.30) | collective-permute-done | bytes 131104 | tf_op jit(solution)/shard_map/ppermute | solution.py:31
  86.2 1.3 collective-permute-start.34
  88.3 1.2 fusion.3
  89.5 2.7 %collective-permute-done.34.refs_1_ = bf16[256,256]{1,0:T(8,128)(2,1)S(1)} collective-permute-done((bf16[256,256]{1,0:T(8,128)(2,1)S(1)}, bf16[256,256]{1,0:T(8,128)(2,1)S(1)}, u32[]{:S(2)}, u32[]{:S(2)}) %collective-permute-start.34) | collective-permute-done | bytes 131104 | tf_op jit(solution)/shard_map/ppermute | solution.py:31
  92.1 1.3 shard_map.154
  94.3 1.2 collective-permute-done.37
  96.4 4.8 %all-to-all-start = ((f16[8,32,768]{2,1,0:T(8,128)(2,1)}), f16[8,32,768]{2,1,0:T(8,128)(2,1)}, u32[]{:S(2)}, u32[]{:S(2)}) async-start(f16[8,32,768]{2,1,0:T(8,128)(2,1)} %bitcast.14), calls=%async_computation | async-start | bytes 786432 | tf_op jit(solution)/shard_map/all_to_all | solution.py:463
  101.2 2.9 %collective-permute-start.38 = (f32[1,512]{1,0:T(1,128)S(1)}, f32[1,512]{1,0:T(1,128)S(1)}, u32[]{:S(2)}, u32[]{:S(2)}) collective-permute-start(f32[1,512]{1,0:T(1,128)S(1)} %add.320), channel_id=1, source_target_pairs={{0,16},{2,18},{4,20},{6,22},{8,24},{10,26},{12,28},{14,30},{16,0},... | collective-permute-start | bytes 6152 | tf_op jit(solution)/shard_map/ppermute | solution.py:31
  104.2 1.5 %fusion.7 = f32[512,512]{1,0:T(8,128)S(1)} fusion(bf16[512,512]{1,0:T(8,128)(2,1)S(1)} %copy-done.20, pred[512,512]{1,0:T(32,128)(4,1)} %broadcast_compare_fusion, bf16[512,256]{1,0:T(8,128)(2,1)S(1)} %get-tuple-element.196, bf16[512,256]{1,0:T(8,128)(2,1)S(1)} %copy-done.3), kind=kOutput, calls=%fused_computation.22 | convolution fusion | flops 403177472 | bytes 2359296 | tf_op jit(solution)/shard_map/dot_general | solution.py:37
  105.7 7.7 %collective-permute-done.38 = f32[1,512]{1,0:T(1,128)S(1)} collective-permute-done((f32[1,512]{1,0:T(1,128)S(1)}, f32[1,512]{1,0:T(1,128)S(1)}, u32[]{:S(2)}, u32[]{:S(2)}) %collective-permute-start.38) | collective-permute-done | bytes 2080 | tf_op jit(solution)/shard_map/ppermute | solution.py:31
  113.4 2.7 %convolution_add_fusion.1 = f32[512,512]{1,0:T(8,128)} fusion(f32[512,512]{1,0:T(8,128)S(1)} %fusion.7, pred[512,512]{1,0:T(32,128)(4,1)S(1)} %copy-done.23, bf16[512,256]{1,0:T(8,128)(2,1)S(1)} %get-tuple-element.196, bf16[512,768]{1,0:T(8,128)(2,1)} %copy-done.21), kind=kOutput, calls=%fused_computation.4 | convolution fusion | flops 403439616 | bytes 3407872 | tf_op jit(solution)/shard_map/dot_general | solution.py:37
  118.8 3.6 %all-to-all-start.1 = ((f16[8,32,768]{2,1,0:T(8,128)(2,1)}), f16[8,32,768]{2,1,0:T(8,128)(2,1)S(1)}, u32[]{:S(2)}, u32[]{:S(2)}) async-start(f16[8,32,768]{2,1,0:T(8,128)(2,1)} %broadcast_in_dim.79), calls=%async_computation.1 | async-start | bytes 786432 | tf_op jit(solution)/shard_map/all_to_all | solution.py:463
  122.5 2.1 %collective-permute-start.40 = (f32[1,512]{1,0:T(1,128)S(1)}, f32[1,512]{1,0:T(1,128)S(1)}, u32[]{:S(2)}, u32[]{:S(2)}) collective-permute-start(f32[1,512]{1,0:T(1,128)S(1)} %add.323), channel_id=1, source_target_pairs={{0,4},{2,6},{4,0},{6,2},{8,12},{10,14},{12,8},{14,10},{16,20},{18,... | collective-permute-start | bytes 6152 | tf_op jit(solution)/shard_map/ppermute | solution.py:31
  124.6 2.9 %collective-permute-done.40 = f32[1,512]{1,0:T(1,128)S(1)} collective-permute-done((f32[1,512]{1,0:T(1,128)S(1)}, f32[1,512]{1,0:T(1,128)S(1)}, u32[]{:S(2)}, u32[]{:S(2)}) %collective-permute-start.40) | collective-permute-done | bytes 2080 | tf_op jit(solution)/shard_map/ppermute | solution.py:31
  128.1 1.3 collective-permute-start.41
  130.4 1.4 %collective-permute-done.41 = f32[1,1024]{1,0:T(1,128)S(1)} collective-permute-done((f32[1,1024]{1,0:T(1,128)S(1)}, f32[1,1024]{1,0:T(1,128)S(1)}, u32[]{:S(2)}, u32[]{:S(2)}) %collective-permute-start.41) | collective-permute-done | bytes 4128 | tf_op jit(solution)/shard_map/ppermute | solution.py:31
  131.9 2.0 %all-to-all-done.1 = f16[8,32,768]{2,1,0:T(8,128)(2,1)S(1)} async-done(((f16[8,32,768]{2,1,0:T(8,128)(2,1)}), f16[8,32,768]{2,1,0:T(8,128)(2,1)S(1)}, u32[]{:S(2)}, u32[]{:S(2)}) %all-to-all-start.1) | async-done | bytes 393248 | tf_op jit(solution)/shard_map/all_to_all | solution.py:463
  134.4 1.5 %collective-permute-done.42 = f16[256,512]{1,0:T(8,128)(2,1)S(1)} collective-permute-done((f16[256,512]{1,0:T(8,128)(2,1)S(1)}, f16[256,512]{1,0:T(8,128)(2,1)S(1)}, u32[]{:S(2)}, u32[]{:S(2)}) %collective-permute-start.42) | collective-permute-done | bytes 262176 | tf_op jit(solution)/shard_map/ppermute | solution.py:31
  (197 shorter events, 30.3 us)
Async XLA Ops:
  3.5 9.5 %collective-permute-start = (f32[256,256]{1,0:T(8,128)S(1)}, f32[256,256]{1,0:T(8,128)S(1)}, u32[]{:S(2)}, u32[]{:S(2)}) collective-permute-start(f32[256,256]{1,0:T(8,128)S(1)} %get-tuple-element.222), channel_id=1, source_target_pairs={{0,1},{1,0},{2,3},{3,2},{4,5},{5,4},{6,7},{7,6},{8,9},{9,8},{10,11... | collective-permute-start | bytes 786440 | tf_op jit(solution)/shard_map/ppermute | solution.py:31
  8.0 1.2 collective-permute-start.1
  9.2 3.7 %collective-permute-start.2 = (s32[2,256]{1,0:T(2,128)S(1)}, s32[2,256]{1,0:T(2,128)S(1)}, u32[]{:S(2)}, u32[]{:S(2)}) collective-permute-start(s32[2,256]{1,0:T(2,128)S(1)} %pad_add_fusion.1), channel_id=1, source_target_pairs={{0,4},{2,6},{4,0},{6,2},{8,12},{10,14},{12,8},{14,10},{16,20},{18,... | collective-permute-start | bytes 6152 | tf_op jit(solution)/shard_map/ppermute | solution.py:31
  13.1 20.2 %copy-start.5 = (bf16[272,256]{1,0:T(8,128)(2,1)}, bf16[272,256]{1,0:T(8,128)(2,1)S(1)}, u32[]{:S(2)}) copy-start(bf16[272,256]{1,0:T(8,128)(2,1)S(1)} %pad_maximum_fusion.refs_0_) | copy-start | bytes 417796
  13.1 6.7 %collective-permute-start.3 = (bf16[272,256]{1,0:T(8,128)(2,1)S(1)}, bf16[272,256]{1,0:T(8,128)(2,1)S(1)}, u32[]{:S(2)}, u32[]{:S(2)}) collective-permute-start(bf16[272,256]{1,0:T(8,128)(2,1)S(1)} %pad_maximum_fusion.refs_0_), channel_id=1, source_target_pairs={{0,8},{2,10},{4,12},{6,14},{8,0},{10,2},{12,4},{14,6},{16,24},{18,... | collective-permute-start | bytes 417800 | tf_op jit(solution)/shard_map/ppermute | solution.py:31
  14.8 13.0 %collective-permute-start.4 = (bf16[272,256]{1,0:T(8,128)(2,1)S(1)}, bf16[272,256]{1,0:T(8,128)(2,1)S(1)}, u32[]{:S(2)}, u32[]{:S(2)}) collective-permute-start(bf16[272,256]{1,0:T(8,128)(2,1)S(1)} %pad_maximum_fusion.refs_0_), channel_id=1, source_target_pairs={{0,16},{2,18},{4,20},{6,22},{8,24},{10,26},{12,28},{14,30},{16,0},... | collective-permute-start | bytes 417800 | tf_op jit(solution)/shard_map/ppermute | solution.py:31
  17.5 10.4 %collective-permute-start.5 = (bf16[272,256]{1,0:T(8,128)(2,1)S(1)}, bf16[272,256]{1,0:T(8,128)(2,1)S(1)}, u32[]{:S(2)}, u32[]{:S(2)}) collective-permute-start(bf16[272,256]{1,0:T(8,128)(2,1)S(1)} %pad_maximum_fusion.refs_0_), channel_id=1, source_target_pairs={{0,24},{2,26},{4,28},{6,30},{8,16},{10,18},{12,20},{14,22},{16,8},... | collective-permute-start | bytes 417800 | tf_op jit(solution)/shard_map/ppermute | solution.py:31
  17.6 10.3 %collective-permute-start.6 = (bf16[272,256]{1,0:T(8,128)(2,1)S(1)}, bf16[272,256]{1,0:T(8,128)(2,1)S(1)}, u32[]{:S(2)}, u32[]{:S(2)}) collective-permute-start(bf16[272,256]{1,0:T(8,128)(2,1)S(1)} %pad_maximum_fusion.refs_0_), channel_id=1, source_target_pairs={{0,4},{2,6},{4,0},{6,2},{8,12},{10,14},{12,8},{14,10},{16,20},{18,... | collective-permute-start | bytes 417800 | tf_op jit(solution)/shard_map/ppermute | solution.py:31
  19.7 8.1 %collective-permute-start.7 = (bf16[272,256]{1,0:T(8,128)(2,1)S(1)}, bf16[272,256]{1,0:T(8,128)(2,1)S(1)}, u32[]{:S(2)}, u32[]{:S(2)}) collective-permute-start(bf16[272,256]{1,0:T(8,128)(2,1)S(1)} %collective-permute-done.3.refs_1_), channel_id=1, source_target_pairs={{0,4},{2,6},{4,0},{6,2},{8,12},{10,14},{12,8},{14,10},{16,20},{18,... | collective-permute-start | bytes 417800 | tf_op jit(solution)/shard_map/ppermute | solution.py:31
  28.2 5.4 %collective-permute-start.10 = (bf16[272,256]{1,0:T(8,128)(2,1)S(1)}, bf16[272,256]{1,0:T(8,128)(2,1)S(1)}, u32[]{:S(2)}, u32[]{:S(2)}) collective-permute-start(bf16[272,256]{1,0:T(8,128)(2,1)S(1)} %pad_maximum_fusion.refs_0_), channel_id=1, source_target_pairs={{0,2},{2,0},{4,6},{6,4},{8,10},{10,8},{12,14},{14,12},{16,18},{18,... | collective-permute-start | bytes 417800 | tf_op jit(solution)/shard_map/ppermute | solution.py:31
  28.3 5.9 %collective-permute-start.11 = (bf16[272,256]{1,0:T(8,128)(2,1)S(1)}, bf16[272,256]{1,0:T(8,128)(2,1)}, u32[]{:S(2)}, u32[]{:S(2)}) collective-permute-start(bf16[272,256]{1,0:T(8,128)(2,1)S(1)} %collective-permute-done.3.refs_1_), channel_id=1, source_target_pairs={{0,2},{2,0},{4,6},{6,4},{8,10},{10,8},{12,14},{14,12},{16,18},{18,... | collective-permute-start | bytes 417800 | tf_op jit(solution)/shard_map/ppermute | solution.py:31
  28.8 7.0 %collective-permute-start.8 = (bf16[272,256]{1,0:T(8,128)(2,1)S(1)}, bf16[272,256]{1,0:T(8,128)(2,1)}, u32[]{:S(2)}, u32[]{:S(2)}) collective-permute-start(bf16[272,256]{1,0:T(8,128)(2,1)S(1)} %collective-permute-done.4.refs_0_), channel_id=1, source_target_pairs={{0,4},{2,6},{4,0},{6,2},{8,12},{10,14},{12,8},{14,10},{16,20},{18,... | collective-permute-start | bytes 417800 | tf_op jit(solution)/shard_map/ppermute | solution.py:31
  30.3 7.3 %collective-permute-start.9 = (bf16[272,256]{1,0:T(8,128)(2,1)S(1)}, bf16[272,256]{1,0:T(8,128)(2,1)}, u32[]{:S(2)}, u32[]{:S(2)}) collective-permute-start(bf16[272,256]{1,0:T(8,128)(2,1)S(1)} %collective-permute-done.5.refs_1_), channel_id=1, source_target_pairs={{0,4},{2,6},{4,0},{6,2},{8,12},{10,14},{12,8},{14,10},{16,20},{18,... | collective-permute-start | bytes 417800 | tf_op jit(solution)/shard_map/ppermute | solution.py:31
  30.8 7.2 %collective-permute-start.16 = (bf16[272,256]{1,0:T(8,128)(2,1)S(1)}, bf16[272,256]{1,0:T(8,128)(2,1)}, u32[]{:S(2)}, u32[]{:S(2)}) collective-permute-start(bf16[272,256]{1,0:T(8,128)(2,1)S(1)} %collective-permute-done.4.refs_0_), channel_id=1, source_target_pairs={{0,2},{2,0},{4,6},{6,4},{8,10},{10,8},{12,14},{14,12},{16,18},{18,... | collective-permute-start | bytes 417800 | tf_op jit(solution)/shard_map/ppermute | solution.py:31
  33.6 5.9 %collective-permute-start.17 = (bf16[272,256]{1,0:T(8,128)(2,1)S(1)}, bf16[272,256]{1,0:T(8,128)(2,1)S(1)}, u32[]{:S(2)}, u32[]{:S(2)}) collective-permute-start(bf16[272,256]{1,0:T(8,128)(2,1)S(1)} %collective-permute-done.5.refs_1_), channel_id=1, source_target_pairs={{0,2},{2,0},{4,6},{6,4},{8,10},{10,8},{12,14},{14,12},{16,18},{18,... | collective-permute-start | bytes 417800 | tf_op jit(solution)/shard_map/ppermute | solution.py:31
  37.6 4.4 %collective-permute-start.14 = (bf16[272,256]{1,0:T(8,128)(2,1)S(1)}, bf16[272,256]{1,0:T(8,128)(2,1)S(1)}, u32[]{:S(2)}, u32[]{:S(2)}) collective-permute-start(bf16[272,256]{1,0:T(8,128)(2,1)S(1)} %collective-permute-done.6.refs_0_), channel_id=1, source_target_pairs={{0,2},{2,0},{4,6},{6,4},{8,10},{10,8},{12,14},{14,12},{16,18},{18,... | collective-permute-start | bytes 417800 | tf_op jit(solution)/shard_map/ppermute | solution.py:31
  37.6 4.4 %collective-permute-start.15 = (bf16[272,256]{1,0:T(8,128)(2,1)S(1)}, bf16[272,256]{1,0:T(8,128)(2,1)S(1)}, u32[]{:S(2)}, u32[]{:S(2)}) collective-permute-start(bf16[272,256]{1,0:T(8,128)(2,1)S(1)} %collective-permute-done.7.refs_1_), channel_id=1, source_target_pairs={{0,2},{2,0},{4,6},{6,4},{8,10},{10,8},{12,14},{14,12},{16,18},{18,... | collective-permute-start | bytes 417800 | tf_op jit(solution)/shard_map/ppermute | solution.py:31
  38.1 6.4 %collective-permute-start.12 = (bf16[272,256]{1,0:T(8,128)(2,1)}, bf16[272,256]{1,0:T(8,128)(2,1)S(1)}, u32[]{:S(2)}, u32[]{:S(2)}) collective-permute-start(bf16[272,256]{1,0:T(8,128)(2,1)} %collective-permute-done.8.refs_0_), channel_id=1, source_target_pairs={{0,2},{2,0},{4,6},{6,4},{8,10},{10,8},{12,14},{14,12},{16,18},{18,... | collective-permute-start | bytes 417800 | tf_op jit(solution)/shard_map/ppermute | solution.py:31
  38.1 6.4 %collective-permute-start.13 = (bf16[272,256]{1,0:T(8,128)(2,1)}, bf16[272,256]{1,0:T(8,128)(2,1)S(1)}, u32[]{:S(2)}, u32[]{:S(2)}) collective-permute-start(bf16[272,256]{1,0:T(8,128)(2,1)} %collective-permute-done.9.refs_1_), channel_id=1, source_target_pairs={{0,2},{2,0},{4,6},{6,4},{8,10},{10,8},{12,14},{14,12},{16,18},{18,... | collective-permute-start | bytes 417800 | tf_op jit(solution)/shard_map/ppermute | solution.py:31
  45.3 3.7 %collective-permute-start.18 = (f32[2,1024]{1,0:T(2,128)S(1)}, f32[2,1024]{1,0:T(2,128)S(1)}, u32[]{:S(2)}, u32[]{:S(2)}) collective-permute-start(f32[2,1024]{1,0:T(2,128)S(1)} %shard_map.143.refs_0_), channel_id=1, source_target_pairs={{0,1},{1,0},{2,3},{3,2},{4,5},{5,4},{6,7},{7,6},{8,9},{9,8},{10,11... | collective-permute-start | bytes 24584 | tf_op jit(solution)/shard_map/ppermute | solution.py:31
  50.5 2.9 %collective-permute-start.21 = (f32[256,256]{1,0:T(8,128)S(1)}, f32[256,256]{1,0:T(8,128)S(1)}, u32[]{:S(2)}, u32[]{:S(2)}) collective-permute-start(f32[256,256]{1,0:T(8,128)S(1)} %get-tuple-element.147), channel_id=1, source_target_pairs={{0,2},{2,0},{4,6},{6,4},{8,10},{10,8},{12,14},{14,12},{16,18},{18,... | collective-permute-start | bytes 786440 | tf_op jit(solution)/shard_map/ppermute | solution.py:31
  50.7 2.6 %collective-permute-start.22 = (f32[256,256]{1,0:T(8,128)S(1)}, f32[256,256]{1,0:T(8,128)S(1)}, u32[]{:S(2)}, u32[]{:S(2)}) collective-permute-start(f32[256,256]{1,0:T(8,128)S(1)} %get-tuple-element.148), channel_id=1, source_target_pairs={{0,2},{2,0},{4,6},{6,4},{8,10},{10,8},{12,14},{14,12},{16,18},{18,... | collective-permute-start | bytes 786440 | tf_op jit(solution)/shard_map/ppermute | solution.py:31
  52.7 4.6 %collective-permute-start.19 = (f32[256,256]{1,0:T(8,128)S(1)}, f32[256,256]{1,0:T(8,128)S(1)}, u32[]{:S(2)}, u32[]{:S(2)}) collective-permute-start(f32[256,256]{1,0:T(8,128)S(1)} %get-tuple-element.145), channel_id=1, source_target_pairs={{0,2},{2,0},{4,6},{6,4},{8,10},{10,8},{12,14},{14,12},{16,18},{18,... | collective-permute-start | bytes 786440 | tf_op jit(solution)/shard_map/ppermute | solution.py:31
  52.9 4.4 %collective-permute-start.20 = (f32[256,256]{1,0:T(8,128)S(1)}, f32[256,256]{1,0:T(8,128)S(1)}, u32[]{:S(2)}, u32[]{:S(2)}) collective-permute-start(f32[256,256]{1,0:T(8,128)S(1)} %get-tuple-element.146), channel_id=1, source_target_pairs={{0,2},{2,0},{4,6},{6,4},{8,10},{10,8},{12,14},{14,12},{16,18},{18,... | collective-permute-start | bytes 786440 | tf_op jit(solution)/shard_map/ppermute | solution.py:31
  55.8 8.7 %collective-permute-start.28 = (f16[512,256]{1,0:T(8,128)(2,1)S(1)}, f16[512,256]{1,0:T(8,128)(2,1)S(1)}, u32[]{:S(2)}, u32[]{:S(2)}) collective-permute-start(f16[512,256]{1,0:T(8,128)(2,1)S(1)} %fusion.12), channel_id=1, source_target_pairs={{0,4},{2,6},{4,0},{6,2},{8,12},{10,14},{12,8},{14,10},{16,20},{18,... | collective-permute-start | bytes 786440 | tf_op jit(solution)/shard_map/ppermute | solution.py:31
  61.0 3.9 %collective-permute-start.26 = (f32[256,256]{1,0:T(8,128)S(1)}, f32[256,256]{1,0:T(8,128)S(1)}, u32[]{:S(2)}, u32[]{:S(2)}) collective-permute-start(f32[256,256]{1,0:T(8,128)S(1)} %get-tuple-element.166), channel_id=1, source_target_pairs={{0,2},{2,0},{4,6},{6,4},{8,10},{10,8},{12,14},{14,12},{16,18},{18,... | collective-permute-start | bytes 786440 | tf_op jit(solution)/shard_map/ppermute | solution.py:31
  61.1 5.1 %collective-permute-start.27 = (f32[256,256]{1,0:T(8,128)S(1)}, f32[256,256]{1,0:T(8,128)S(1)}, u32[]{:S(2)}, u32[]{:S(2)}) collective-permute-start(f32[256,256]{1,0:T(8,128)S(1)} %get-tuple-element.167), channel_id=1, source_target_pairs={{0,2},{2,0},{4,6},{6,4},{8,10},{10,8},{12,14},{14,12},{16,18},{18,... | collective-permute-start | bytes 786440 | tf_op jit(solution)/shard_map/ppermute | solution.py:31
  61.6 8.3 %collective-permute-start.25 = (f16[512,256]{1,0:T(8,128)(2,1)S(1)}, f16[512,256]{1,0:T(8,128)(2,1)S(1)}, u32[]{:S(2)}, u32[]{:S(2)}) collective-permute-start(f16[512,256]{1,0:T(8,128)(2,1)S(1)} %fusion.13), channel_id=1, source_target_pairs={{0,4},{2,6},{4,0},{6,2},{8,12},{10,14},{12,8},{14,10},{16,20},{18,... | collective-permute-start | bytes 786440 | tf_op jit(solution)/shard_map/ppermute | solution.py:31
  64.3 5.5 %collective-permute-start.23 = (f32[256,256]{1,0:T(8,128)S(1)}, f32[256,256]{1,0:T(8,128)S(1)}, u32[]{:S(2)}, u32[]{:S(2)}) collective-permute-start(f32[256,256]{1,0:T(8,128)S(1)} %get-tuple-element.163), channel_id=1, source_target_pairs={{0,2},{2,0},{4,6},{6,4},{8,10},{10,8},{12,14},{14,12},{16,18},{18,... | collective-permute-start | bytes 786440 | tf_op jit(solution)/shard_map/ppermute | solution.py:31
  64.4 5.4 %collective-permute-start.24 = (f32[256,256]{1,0:T(8,128)S(1)}, f32[256,256]{1,0:T(8,128)S(1)}, u32[]{:S(2)}, u32[]{:S(2)}) collective-permute-start(f32[256,256]{1,0:T(8,128)S(1)} %get-tuple-element.164), channel_id=1, source_target_pairs={{0,2},{2,0},{4,6},{6,4},{8,10},{10,8},{12,14},{14,12},{16,18},{18,... | collective-permute-start | bytes 786440 | tf_op jit(solution)/shard_map/ppermute | solution.py:31
  64.9 21.2 %collective-permute-start.32 = (bf16[256,768]{1,0:T(8,128)(2,1)S(1)}, bf16[256,768]{1,0:T(8,128)(2,1)S(1)}, u32[]{:S(2)}, u32[]{:S(2)}) collective-permute-start(bf16[256,768]{1,0:T(8,128)(2,1)S(1)} %copy-done.22), channel_id=1, source_target_pairs={{0,1},{1,0},{2,3},{3,2},{4,5},{5,4},{6,7},{7,6},{8,9},{9,8},{10,11... | collective-permute-start | bytes 1179656 | tf_op jit(solution)/shard_map/ppermute | solution.py:31
  71.4 8.1 %collective-permute-start.29 = (f16[256,256]{1,0:T(8,128)(2,1)S(1)}, f16[256,256]{1,0:T(8,128)(2,1)S(1)}, u32[]{:S(2)}, u32[]{:S(2)}) collective-permute-start(f16[256,256]{1,0:T(8,128)(2,1)S(1)} %get-tuple-element.224), channel_id=1, source_target_pairs={{0,24},{2,26},{4,28},{6,30},{8,16},{10,18},{12,20},{14,22},{16,8},... | collective-permute-start | bytes 393224 | tf_op jit(solution)/shard_map/ppermute | solution.py:31
  73.9 12.1 %collective-permute-start.30 = (f16[256,256]{1,0:T(8,128)(2,1)S(1)}, f16[256,256]{1,0:T(8,128)(2,1)S(1)}, u32[]{:S(2)}, u32[]{:S(2)}) collective-permute-start(f16[256,256]{1,0:T(8,128)(2,1)S(1)} %get-tuple-element.225), channel_id=1, source_target_pairs={{0,16},{2,18},{4,20},{6,22},{8,24},{10,26},{12,28},{14,30},{16,0},... | collective-permute-start | bytes 393224 | tf_op jit(solution)/shard_map/ppermute | solution.py:31
  75.0 11.0 %collective-permute-start.31 = (f16[256,256]{1,0:T(8,128)(2,1)S(1)}, f16[256,256]{1,0:T(8,128)(2,1)S(1)}, u32[]{:S(2)}, u32[]{:S(2)}) collective-permute-start(f16[256,256]{1,0:T(8,128)(2,1)S(1)} %get-tuple-element.242), channel_id=1, source_target_pairs={{0,8},{2,10},{4,12},{6,14},{8,0},{10,2},{12,4},{14,6},{16,24},{18,... | collective-permute-start | bytes 393224 | tf_op jit(solution)/shard_map/ppermute | solution.py:31
  75.9 10.3 %collective-permute-start.33 = (f32[1,512]{1,0:T(1,128)S(1)}, f32[1,512]{1,0:T(1,128)S(1)}, u32[]{:S(2)}, u32[]{:S(2)}) collective-permute-start(f32[1,512]{1,0:T(1,128)S(1)} %bitcast.127), channel_id=1, source_target_pairs={{0,1},{1,0},{2,3},{3,2},{4,5},{5,4},{6,7},{7,6},{8,9},{9,8},{10,11... | collective-permute-start | bytes 6152 | tf_op jit(solution)/shard_map/ppermute | solution.py:31
  86.1 1.8 %collective-permute-start.35 = (bf16[256,768]{1,0:T(8,128)(2,1)S(1)}, bf16[256,768]{1,0:T(8,128)(2,1)S(1)}, u32[]{:S(2)}, u32[]{:S(2)}) collective-permute-start(bf16[256,768]{1,0:T(8,128)(2,1)S(1)} %collective-permute-done.32), channel_id=1, source_target_pairs={{0,2},{2,0},{4,6},{6,4},{8,10},{10,8},{12,14},{14,12},{16,18},{18,... | collective-permute-start | bytes 1179656 | tf_op jit(solution)/shard_map/ppermute | solution.py:31
  86.2 5.9 %collective-permute-start.34 = (bf16[256,256]{1,0:T(8,128)(2,1)S(1)}, bf16[256,256]{1,0:T(8,128)(2,1)S(1)}, u32[]{:S(2)}, u32[]{:S(2)}) collective-permute-start(bf16[256,256]{1,0:T(8,128)(2,1)S(1)} %add_convert_fusion.1.refs_0_), channel_id=1, source_target_pairs={{0,1},{1,0},{2,3},{3,2},{4,5},{5,4},{6,7},{7,6},{8,9},{9,8},{10,11... | collective-permute-start | bytes 393224 | tf_op jit(solution)/shard_map/ppermute | solution.py:31
  93.7 1.8 %collective-permute-start.36 = (f16[256,768]{1,0:T(8,128)(2,1)S(1)}, f16[256,768]{1,0:T(8,128)(2,1)S(1)}, u32[]{:S(2)}, u32[]{:S(2)}) collective-permute-start(f16[256,768]{1,0:T(8,128)(2,1)S(1)} %dynamic-slice_convert_fusion), channel_id=1, source_target_pairs={{0,2},{2,0},{4,6},{6,4},{8,10},{10,8},{12,14},{14,12},{16,18},{18,... | collective-permute-start | bytes 1179656 | tf_op jit(solution)/shard_map/ppermute | solution.py:31
  93.8 1.7 %collective-permute-start.37 = (f32[1,512]{1,0:T(1,128)S(1)}, f32[1,512]{1,0:T(1,128)S(1)}, u32[]{:S(2)}, u32[]{:S(2)}) collective-permute-start(f32[1,512]{1,0:T(1,128)S(1)} %get-tuple-element.193), channel_id=1, source_target_pairs={{0,2},{2,0},{4,6},{6,4},{8,10},{10,8},{12,14},{14,12},{16,18},{18,... | collective-permute-start | bytes 6152 | tf_op jit(solution)/shard_map/ppermute | solution.py:31
  96.4 17.0 %copy-start.23 = (pred[512,512]{1,0:T(32,128)(4,1)S(1)}, pred[512,512]{1,0:T(32,128)(4,1)}, u32[]{:S(2)}) copy-start(pred[512,512]{1,0:T(32,128)(4,1)} %fusion.3) | copy-start | bytes 786436
  96.4 20.5 %all-to-all-start = ((f16[8,32,768]{2,1,0:T(8,128)(2,1)}), f16[8,32,768]{2,1,0:T(8,128)(2,1)}, u32[]{:S(2)}, u32[]{:S(2)}) async-start(f16[8,32,768]{2,1,0:T(8,128)(2,1)} %bitcast.14), calls=%async_computation | async-start | bytes 786432 | tf_op jit(solution)/shard_map/all_to_all | solution.py:463
  101.2 12.1 %collective-permute-start.38 = (f32[1,512]{1,0:T(1,128)S(1)}, f32[1,512]{1,0:T(1,128)S(1)}, u32[]{:S(2)}, u32[]{:S(2)}) collective-permute-start(f32[1,512]{1,0:T(1,128)S(1)} %add.320), channel_id=1, source_target_pairs={{0,16},{2,18},{4,20},{6,22},{8,24},{10,26},{12,28},{14,30},{16,0},... | collective-permute-start | bytes 6152 | tf_op jit(solution)/shard_map/ppermute | solution.py:31
  113.4 3.6 %collective-permute-start.39 = (f32[1,512]{1,0:T(1,128)S(1)}, f32[1,512]{1,0:T(1,128)S(1)}, u32[]{:S(2)}, u32[]{:S(2)}) collective-permute-start(f32[1,512]{1,0:T(1,128)S(1)} %add.322), channel_id=1, source_target_pairs={{0,8},{2,10},{4,12},{6,14},{8,0},{10,2},{12,4},{14,6},{16,24},{18,... | collective-permute-start | bytes 6152 | tf_op jit(solution)/shard_map/ppermute | solution.py:31
  118.8 15.0 %all-to-all-start.1 = ((f16[8,32,768]{2,1,0:T(8,128)(2,1)}), f16[8,32,768]{2,1,0:T(8,128)(2,1)S(1)}, u32[]{:S(2)}, u32[]{:S(2)}) async-start(f16[8,32,768]{2,1,0:T(8,128)(2,1)} %broadcast_in_dim.79), calls=%async_computation.1 | async-start | bytes 786432 | tf_op jit(solution)/shard_map/all_to_all | solution.py:463
  122.5 5.0 %collective-permute-start.40 = (f32[1,512]{1,0:T(1,128)S(1)}, f32[1,512]{1,0:T(1,128)S(1)}, u32[]{:S(2)}, u32[]{:S(2)}) collective-permute-start(f32[1,512]{1,0:T(1,128)S(1)} %add.323), channel_id=1, source_target_pairs={{0,4},{2,6},{4,0},{6,2},{8,12},{10,14},{12,8},{14,10},{16,20},{18,... | collective-permute-start | bytes 6152 | tf_op jit(solution)/shard_map/ppermute | solution.py:31
  128.1 3.8 %collective-permute-start.41 = (f32[1,1024]{1,0:T(1,128)S(1)}, f32[1,1024]{1,0:T(1,128)S(1)}, u32[]{:S(2)}, u32[]{:S(2)}) collective-permute-start(f32[1,1024]{1,0:T(1,128)S(1)} %bitcast.105), channel_id=1, source_target_pairs={{0,1},{1,0},{2,3},{3,2},{4,5},{5,4},{6,7},{7,6},{8,9},{9,8},{10,11... | collective-permute-start | bytes 12296 | tf_op jit(solution)/shard_map/ppermute | solution.py:31
  129.5 6.4 %collective-permute-start.42 = (f16[256,512]{1,0:T(8,128)(2,1)S(1)}, f16[256,512]{1,0:T(8,128)(2,1)S(1)}, u32[]{:S(2)}, u32[]{:S(2)}) collective-permute-start(f16[256,512]{1,0:T(8,128)(2,1)S(1)} %multiply_convert_fusion), channel_id=1, source_target_pairs={{0,1},{1,0},{2,3},{3,2},{4,5},{5,4},{6,7},{7,6},{8,9},{9,8},{10,11... | collective-permute-start | bytes 786440 | tf_op jit(solution)/shard_map/ppermute | solution.py:31
  133.8 3.4 %collective-permute-start.43 = (f16[256,768]{1,0:T(8,128)(2,1)S(1)}, f16[256,768]{1,0:T(8,128)(2,1)S(1)}, u32[]{:S(2)}, u32[]{:S(2)}) collective-permute-start(f16[256,768]{1,0:T(8,128)(2,1)S(1)} %bitcast.102), channel_id=1, source_target_pairs={{0,2},{2,0},{4,6},{6,4},{8,10},{10,8},{12,14},{14,12},{16,18},{18,... | collective-permute-start | bytes 1179656 | tf_op jit(solution)/shard_map/ppermute | solution.py:31
  (27 other events, 181.2 us)
